TPU v7x, 1024 devices: a whole 4x8x16 slice. The times are simulated.
1024 devices in a mesh: dp: 16 (over z), expert: 64 (over x, y, core).
Axes of the slice: x: 4, y: 8, z: 16, core: 2. Of those that a mesh axis runs over, the one named last changes fastest.
Arguments:
- acts: bfloat16 [1024, 4096], P('expert', 'dp'), may hold values from -6 to 6
- grad_out: bfloat16 [1024, 4096], P('expert', 'dp'), may hold values from -18 to 18
- routes: int32 [1024, 8], P('expert'), may hold values from 0 to 63, all different within a row; in each aligned block of 16 rows (0 to 15, 16 to 31, ...) at most 3 rows name the same one
- combine: float32 [1024, 8], P('expert'), may hold values from 0.05 to 0.4
- w_gate: bfloat16 [64, 4096, 768], P('expert', 'dp'), may hold values from -0.09375 to 0.09375
- w_up: bfloat16 [64, 4096, 768], P('expert', 'dp'), may hold values from -0.09375 to 0.09375
- w_down: bfloat16 [64, 768, 4096], P('expert', None, 'dp'), may hold values from -0.21875 to 0.21875
Outputs:
- grad_acts: bfloat16 [1024, 4096], P('expert', 'dp')
- grad_gate_w: bfloat16 [64, 4096, 768], P('expert', 'dp')
- grad_up_w: bfloat16 [64, 4096, 768], P('expert', 'dp')
- grad_down_w: bfloat16 [64, 768, 4096], P('expert', None, 'dp')
Inputs may be any that keep to these rules, and one draw needn't show every extreme that they name: `routes`: each row names 8 different experts. Among the rows of one index of the expert axis (aligned blocks of 16 tokens), no expert is named by more than 3 rows, a bound that some block reaches.
All inputs are finite; a program needn't handle non-finite values.
Results may differ from a plain program's by a relative error of at most 0.0064.
Values may be sent and summed in bfloat16 or wider, within the bound.
No kernel may reach another device: no remote copies, remote signals or barrier semaphores. Data moves between devices by JAX's collectives and lax.ppermute only.
A program may use at most 32 MiB of HBM per device.

v0:
```python
import jax
import jax.numpy as jnp
from jax import lax
from jax.sharding import PartitionSpec as P


def activate(pre_gate, pre_up, hidden_grad):
    sigmoid_gate = jax.nn.sigmoid(pre_gate)
    silu_gate = pre_gate * sigmoid_gate
    hidden = (silu_gate * pre_up).astype(jnp.bfloat16)
    up_grad = (hidden_grad * silu_gate).astype(jnp.bfloat16)
    gate_grad = (
        hidden_grad * pre_up * sigmoid_gate * (1.0 + pre_gate * (1.0 - sigmoid_gate))
    ).astype(jnp.bfloat16)
    return (hidden, gate_grad, up_grad)


def on_device(acts, grad_out, routes, combine, w_gate, w_up, w_down):
    tok_count, local_width = acts.shape
    picks = routes.shape[1]
    experts = lax.axis_size("expert")
    capacity = min(tok_count, max(2, 3 * tok_count * picks // (2 * experts)))
    slot_rows = experts * capacity
    flat_ids = routes.reshape(-1)
    onehot = (flat_ids[:, None] == jnp.arange(experts, dtype=jnp.int32)[None, :]).astype(jnp.int32)
    ranking = jnp.sum((jnp.cumsum(onehot, axis=0) - 1) * onehot, axis=1)
    slot_index = flat_ids * capacity + ranking
    dispatch = (slot_index[:, None] == jnp.arange(slot_rows, dtype=jnp.int32)[None, :]).astype(
        jnp.bfloat16
    )
    repeated = jnp.repeat(acts, picks, axis=0)
    scaled = (combine[:, :, None] * grad_out[:, None, :].astype(jnp.float32)).astype(jnp.bfloat16)
    scaled = scaled.reshape(tok_count * picks, local_width)
    send_x = jnp.einsum("rs,rd->sd", dispatch, repeated, preferred_element_type=jnp.float32).astype(
        jnp.bfloat16
    )
    send_dy = jnp.einsum("rs,rd->sd", dispatch, scaled, preferred_element_type=jnp.float32).astype(
        jnp.bfloat16
    )
    recv_x, recv_dy = (
        lax.all_to_all(
            send_x.reshape(experts, capacity, local_width),
            "expert",
            split_axis=0,
            concat_axis=0,
            tiled=True,
        ),
        lax.all_to_all(
            send_dy.reshape(experts, capacity, local_width),
            "expert",
            split_axis=0,
            concat_axis=0,
            tiled=True,
        ),
    )
    rows_x = recv_x.reshape(slot_rows, local_width)
    rows_dy = recv_dy.reshape(slot_rows, local_width)
    gate_w = w_gate[0]
    up_w = w_up[0]
    down_w = w_down[0]
    term_full = jnp.stack(
        [
            jnp.dot(rows_x, gate_w, preferred_element_type=jnp.float32),
            jnp.dot(rows_x, up_w, preferred_element_type=jnp.float32),
            jnp.einsum("rd,fd->rf", rows_dy, down_w, preferred_element_type=jnp.float32),
        ],
        axis=1,
    )
    sums = lax.psum_scatter(term_full, "dp", scatter_dimension=2, tiled=True)
    hidden, gate_grad, up_grad = activate(sums[:, 0], sums[:, 1], sums[:, 2])
    packed = jnp.stack([hidden, gate_grad, up_grad], axis=1)
    block_in = lax.all_gather(packed, "dp", axis=2, tiled=True)
    new_gate = jnp.einsum("rd,rf->df", rows_x, block_in[:, 1], preferred_element_type=jnp.float32)
    new_up = jnp.einsum("rd,rf->df", rows_x, block_in[:, 2], preferred_element_type=jnp.float32)
    new_down = jnp.einsum("rf,rd->fd", block_in[:, 0], rows_dy, preferred_element_type=jnp.float32)
    new_rows = jnp.einsum(
        "rf,df->rd", block_in[:, 1], gate_w, preferred_element_type=jnp.float32
    ) + jnp.einsum("rf,df->rd", block_in[:, 2], up_w, preferred_element_type=jnp.float32)
    row_grads = new_rows.astype(jnp.bfloat16).reshape(experts, capacity, local_width)
    returned = lax.all_to_all(row_grads, "expert", split_axis=0, concat_axis=0, tiled=True).reshape(
        slot_rows, local_width
    )
    per_pick = jnp.dot(dispatch, returned, preferred_element_type=jnp.float32).reshape(
        tok_count, picks, local_width
    )
    grad_acts = jnp.sum(per_pick, axis=1).astype(jnp.bfloat16)
    return (
        grad_acts,
        new_gate.astype(jnp.bfloat16)[None],
        new_up.astype(jnp.bfloat16)[None],
        new_down.astype(jnp.bfloat16)[None],
    )


def solution(mesh):
    return jax.shard_map(
        on_device,
        mesh=mesh,
        in_specs=(
            P("expert", "dp"),
            P("expert", "dp"),
            P("expert", None),
            P("expert", None),
            P("expert", "dp", None),
            P("expert", "dp", None),
            P("expert", None, "dp"),
        ),
        out_specs=(
            P("expert", "dp"),
            P("expert", "dp", None),
            P("expert", "dp", None),
            P("expert", None, "dp"),
        ),
        check_vma=False,
    )
```

profile of v0, /device:TPU:1, one launch (start us, length us, event | category | flops | bytes accessed | tf_op | source)
XLA Modules:
  0.0 277.3 jit_solution(7141480387138640970)
XLA Ops:
  7.2 0.8 copy.22
  8.6 1.0 convolution_convert_fusion.4
  9.6 0.7 reshape.72
  10.3 18.2 %all-to-all-start = ((bf16[64,3,256]{2,1,0:T(4,128)(2,1)}), bf16[64,3,256]{2,1,0:T(4,128)(2,1)S(1)}, u32[]{:S(2)}, u32[]{:S(2)}) async-start(bf16[64,3,256]{2,1,0:T(4,128)(2,1)} %reshape.72), calls=%async_computation | async-start | bytes 262144 | tf_op jit(solution)/shard_map/all_to_all | solution.py:41
  28.5 0.7 convert_element_type.47
  29.2 0.8 copy.24
  30.0 0.3 convolution_convert_fusion.3
  30.4 0.7 reshape.74
  31.1 7.9 %all-to-all-done = bf16[64,3,256]{2,1,0:T(4,128)(2,1)S(1)} async-done(((bf16[64,3,256]{2,1,0:T(4,128)(2,1)}), bf16[64,3,256]{2,1,0:T(4,128)(2,1)S(1)}, u32[]{:S(2)}, u32[]{:S(2)}) %all-to-all-start) | async-done | bytes 98336 | tf_op jit(solution)/shard_map/all_to_all | solution.py:41
  39.0 4.9 %all-to-all-start.1 = ((bf16[64,3,256]{2,1,0:T(4,128)(2,1)}), bf16[64,3,256]{2,1,0:T(4,128)(2,1)S(1)}, u32[]{:S(2)}, u32[]{:S(2)}) async-start(bf16[64,3,256]{2,1,0:T(4,128)(2,1)} %reshape.74), calls=%async_computation.1 | async-start | bytes 262144 | tf_op jit(solution)/shard_map/all_to_all | solution.py:48
  44.5 9.7 %all-to-all-done.1 = bf16[64,3,256]{2,1,0:T(4,128)(2,1)S(1)} async-done(((bf16[64,3,256]{2,1,0:T(4,128)(2,1)}), bf16[64,3,256]{2,1,0:T(4,128)(2,1)S(1)}, u32[]{:S(2)}, u32[]{:S(2)}) %all-to-all-start.1) | async-done | bytes 98336 | tf_op jit(solution)/shard_map/all_to_all | solution.py:48
  54.7 2.8 copy.25
  57.6 1.3 dynamic-slice
  59.5 142.1 %all-reduce.3.cloned.1.call-done = f32[192,3,768]{0,1,2:T(4,128)} async-done(((f32[192,3,768]{0,1,2:T(4,128)}), f32[192,3,768]{0,1,2:T(4,128)}) %all-reduce.3.cloned.1.call-update) | async-done | bytes 1769488
  201.7 1.2 constant_dynamic-slice_fusion
  203.0 28.2 %all_gather.3 = bf16[192,3,768]{0,2,1:T(8,128)(2,1)S(1)} all-gather(bf16[192,3,48]{0,2,1:T(8,128)(2,1)S(1)} %pad_maximum_fusion.1), channel_id=1, replica_groups=mesh['dp'=16,'expert'=64] {'dp'}, dimensions={2}, use_global_device_ids=true | all-gather | bytes 940032 | tf_op jit(solution)/shard_map/all_gather | solution.py:72
  231.3 1.1 fusion
  232.6 0.3 fusion.3
  232.9 0.7 reshape.76
  233.6 25.5 %all-to-all-start.2 = ((bf16[64,3,256]{2,1,0:T(4,128)(2,1)}), bf16[64,3,256]{2,1,0:T(4,128)(2,1)S(1)}, u32[]{:S(2)}, u32[]{:S(2)}) async-start(bf16[64,3,256]{2,1,0:T(4,128)(2,1)} %reshape.76), calls=%async_computation.2 | async-start | bytes 262144 | tf_op jit(solution)/shard_map/all_to_all | solution.py:80
  259.2 1.1 fusion.1
  260.2 1.0 fusion.2
  261.2 8.3 %all-to-all-done.2 = bf16[64,3,256]{2,1,0:T(4,128)(2,1)S(1)} async-done(((bf16[64,3,256]{2,1,0:T(4,128)(2,1)}), bf16[64,3,256]{2,1,0:T(4,128)(2,1)S(1)}, u32[]{:S(2)}, u32[]{:S(2)}) %all-to-all-start.2) | async-done | bytes 98336 | tf_op jit(solution)/shard_map/all_to_all | solution.py:80
  269.6 0.8 convolution_reduce_fusion
  (28 shorter events, 2.3 us)
Async XLA Ops:
  7.2 37.1 %copy-start = (bf16[1,256,768]{2,1,0:T(8,128)(2,1)S(1)}, bf16[1,256,768]{2,1,0:T(8,128)(2,1)}, u32[]{:S(2)}) copy-start(bf16[1,256,768]{2,1,0:T(8,128)(2,1)} %param.11) | copy-start | bytes 1179652
  7.2 36.8 %copy-start.1 = (bf16[1,256,768]{2,1,0:T(8,128)(2,1)S(1)}, bf16[1,256,768]{2,1,0:T(8,128)(2,1)}, u32[]{:S(2)}) copy-start(bf16[1,256,768]{2,1,0:T(8,128)(2,1)} %param.12) | copy-start | bytes 1179652
  10.3 28.7 %all-to-all-start = ((bf16[64,3,256]{2,1,0:T(4,128)(2,1)}), bf16[64,3,256]{2,1,0:T(4,128)(2,1)S(1)}, u32[]{:S(2)}, u32[]{:S(2)}) async-start(bf16[64,3,256]{2,1,0:T(4,128)(2,1)} %reshape.72), calls=%async_computation | async-start | bytes 262144 | tf_op jit(solution)/shard_map/all_to_all | solution.py:41
  39.0 15.2 %all-to-all-start.1 = ((bf16[64,3,256]{2,1,0:T(4,128)(2,1)}), bf16[64,3,256]{2,1,0:T(4,128)(2,1)S(1)}, u32[]{:S(2)}, u32[]{:S(2)}) async-start(bf16[64,3,256]{2,1,0:T(4,128)(2,1)} %reshape.74), calls=%async_computation.1 | async-start | bytes 262144 | tf_op jit(solution)/shard_map/all_to_all | solution.py:48
  43.9 157.8 %all-reduce.3.cloned.1.call-start = ((), (), s32[]{:S(2)}) async-start(), calls=%async_computation.3 | async-start | bytes 6291456
  44.0 10.3 %copy-start.3 = (bf16[1,768,256]{2,1,0:T(8,128)(2,1)S(1)}, bf16[1,768,256]{2,1,0:T(8,128)(2,1)}, u32[]{:S(2)}) copy-start(bf16[1,768,256]{2,1,0:T(8,128)(2,1)} %param.13) | copy-start | bytes 1179652
  231.3 1.4 copy-start.2
  233.6 35.9 %all-to-all-start.2 = ((bf16[64,3,256]{2,1,0:T(4,128)(2,1)}), bf16[64,3,256]{2,1,0:T(4,128)(2,1)S(1)}, u32[]{:S(2)}, u32[]{:S(2)}) async-start(bf16[64,3,256]{2,1,0:T(4,128)(2,1)} %reshape.76), calls=%async_computation.2 | async-start | bytes 262144 | tf_op jit(solution)/shard_map/all_to_all | solution.py:80
Sparse Core Ops, SparseCore 0:
  57.6 144.0 all-reduce.2
where the time goes:
time: 278 us; the launch traced here: 277 us
  waiting for transfers between devices  168 us (60%)
  starting transfers between devices  48.7 us (18%)
  blocking collectives  28.2 us (10%)
  between operations  14.9 us (5%)
  local copies, waits for them, and re-layouts  9.51 us (3%)
  matrix products  6.64 us (2%)
    unnamed x2, waiting for transfers between devices  142 us
    all_gather x1, blocking collectives, on_device(): block_in = lax.all_gather(packed, 'dp', axis=2, tiled=True)  28.2 us
    all_to_all x1, starting transfers between devices, on_device(): lax.all_to_all(row_grads, 'expert', split_axis=0, concat_axis=0, tiled=True)  25.5 us
    all_to_all x1, starting transfers between devices, on_device(): lax.all_to_all(send_x.reshape(experts, capacity, local_width), 'expert',...  18.2 us
    all_to_all x1, waiting for transfers between devices, on_device(): lax.all_to_all(send_dy.reshape(experts, capacity, local_width), 'expert',...  9.7 us
    all_to_all x1, waiting for transfers between devices, on_device(): lax.all_to_all(row_grads, 'expert', split_axis=0, concat_axis=0, tiled=True)  8.31 us
    all_to_all x1, waiting for transfers between devices, on_device(): lax.all_to_all(send_x.reshape(experts, capacity, local_width), 'expert',...  7.91 us
  transfers between devices with their start and end apart: 4, of which 4 were waited for; matrix products, arithmetic and copies ran while one was open for 2% of the time, Pallas kernels for 0%

commit v1 on v0

v1 whole, which is shorter than its diff:
```python
import functools

import jax
import jax.numpy as jnp
from jax import lax
from jax.experimental import pallas as pl
from jax.experimental.pallas import tpu as pltpu
from jax.sharding import PartitionSpec as P

BF16 = jnp.bfloat16
F32 = jnp.float32
TOK = 16
PICKS = 8
EXPERTS = 64
CAP = 3
ROWS = EXPERTS * CAP
WIDTH = 256
HIDDEN = 768
HALF = HIDDEN // 2
PACK = 3 * HALF
GROUP = 4
CHUNK = 24
NEAR = [[GROUP * a + b for b in range(GROUP)] for a in range(GROUP)]
FAR = [[GROUP * a + b for a in range(GROUP)] for b in range(GROUP)]
VMEM_LIMIT = 24 * 1024 * 1024


def dot(a, b, contract):
    return lax.dot_general(a, b, (contract, ((), ())), preferred_element_type=F32)


def iota(shape, dim):
    return lax.broadcasted_iota(jnp.int32, shape, dim)


def column(row):
    diagonal = iota((TOK, TOK), 0) == iota((TOK, TOK), 1)
    spread = jnp.where(diagonal, jnp.broadcast_to(row, (TOK, TOK)), jnp.zeros((), row.dtype))
    return jnp.sum(spread, axis=1, keepdims=True)


def slots_of(routes_t):
    expert = lax.shift_right_logical(iota((TOK, EXPERTS * 8), 1), 3)
    hits = [column(routes_t[k : k + 1, :]) == expert for k in range(PICKS)]
    named = functools.reduce(jnp.logical_or, hits)
    earlier = (iota((TOK, TOK), 0) > iota((TOK, TOK), 1)).astype(F32).astype(BF16)
    rank = dot(earlier, named.astype(F32).astype(BF16), ((1,), (0,))).astype(jnp.int32)
    return hits, named, rank


def as_bf16(mask):
    return mask.astype(F32).astype(BF16)


def dispatch_body(routes_t, combine_t, acts, grad_out):
    hits, named, rank = slots_of(routes_t)
    place = jnp.bitwise_and(iota((TOK, EXPERTS * 8), 1), 7)
    wanted_x = place == rank
    wanted_dy = place == rank + 4
    choose = [as_bf16(named & wanted_x)] + [as_bf16(hit & wanted_dy) for hit in hits]
    wide = grad_out.astype(F32)
    values = [acts] + [(column(combine_t[k : k + 1, :]) * wide).astype(BF16) for k in range(PICKS)]
    choose = jnp.concatenate(choose, axis=0)
    values = jnp.concatenate(values, axis=0)
    return dot(choose, values, ((0,), (0,))).astype(BF16)


def dispatch_kernel(routes_ref, combine_ref, acts_ref, grad_ref, out_ref):
    out_ref[...] = dispatch_body(routes_ref[...], combine_ref[...], acts_ref[...], grad_ref[...])


def rows_body(received):
    row, slot = iota((ROWS, EXPERTS * 8), 0), iota((ROWS, EXPERTS * 8), 1)
    base = jnp.bitwise_and(row, EXPERTS - 1) * 8 + lax.shift_right_logical(row, 6)
    rows_x = dot(as_bf16(slot == base), received, ((1,), (0,))).astype(BF16)
    rows_dy = dot(as_bf16(slot == base + 4), received, ((1,), (0,))).astype(BF16)
    return rows_x, rows_dy


def product_blocks(rows_x, rows_dy, w_gate, w_up, w_down):
    gate = dot(rows_x, w_gate, ((1,), (0,)))
    up = dot(rows_x, w_up, ((1,), (0,)))
    back = dot(rows_dy, w_down, ((1,), (1,)))
    blocks = {}
    for half in range(2):
        cut = slice(half * HALF, (half + 1) * HALF)
        both = jnp.concatenate([gate[:, cut], up[:, cut], back[:, cut]], axis=1)
        for b in range(GROUP):
            low, high = CHUNK * b, CHUNK * (GROUP + b)
            block = jnp.concatenate([both[low : low + CHUNK], both[high : high + CHUNK]], axis=0)
            blocks[b, half] = block.astype(BF16)
    return blocks


def product_kernel(received_ref, w_gate_ref, w_up_ref, w_down_ref, parts_ref, x_ref, dy_ref):
    rows_x, rows_dy = rows_body(received_ref[...])
    x_ref[...] = rows_x
    dy_ref[...] = rows_dy
    blocks = product_blocks(rows_x, rows_dy, w_gate_ref[...], w_up_ref[...], w_down_ref[...])
    for (b, half), block in blocks.items():
        parts_ref[b, 2 * CHUNK * half : 2 * CHUNK * (half + 1), :] = block


def add_body(parts):
    return (parts[0].astype(F32) + parts[1].astype(F32)) + (parts[2].astype(F32) + parts[3].astype(F32))


def add_kernel(parts_ref, out_ref):
    out_ref[...] = add_body(parts_ref[...]).astype(BF16)


def activate_body(parts):
    total = add_body(parts)
    pre_gate, pre_up, hidden_grad = total[:, :HALF], total[:, HALF : 2 * HALF], total[:, 2 * HALF :]
    sigmoid_gate = jax.nn.sigmoid(pre_gate)
    silu_gate = pre_gate * sigmoid_gate
    hidden = silu_gate * pre_up
    up_grad = hidden_grad * silu_gate
    gate_grad = hidden_grad * pre_up * sigmoid_gate * (1.0 + pre_gate * (1.0 - sigmoid_gate))
    return jnp.concatenate([gate_grad, up_grad, hidden], axis=1).astype(BF16)


def activate_kernel(parts_ref, out_ref):
    out_ref[...] = activate_body(parts_ref[...])


def row_grad_body(packed, w_gate, w_up):
    total = jnp.zeros((ROWS, WIDTH), F32)
    for half in range(2):
        cut = slice(half * HALF, (half + 1) * HALF)
        total += dot(packed[half][:, :HALF], w_gate[:, cut], ((1,), (1,)))
        total += dot(packed[half][:, HALF : 2 * HALF], w_up[:, cut], ((1,), (1,)))
    rounded = total.astype(BF16)
    slot, row = iota((EXPERTS * 8, ROWS), 0), iota((EXPERTS * 8, ROWS), 1)
    base = jnp.bitwise_and(row, EXPERTS - 1) * 8 + lax.shift_right_logical(row, 6) * 2
    left = dot(as_bf16(slot == base), rounded[:, :128], ((1,), (0,)))
    right = dot(as_bf16(slot == base + 1), rounded[:, 128:], ((1,), (0,)))
    return (left + right).astype(BF16)


def row_grad_kernel(packed_ref, w_gate_ref, w_up_ref, out_ref):
    out_ref[...] = row_grad_body(packed_ref[...], w_gate_ref[...], w_up_ref[...])


def weight_kernel(packed_ref, x_ref, dy_ref, gate_ref, up_ref, down_ref):
    rows_x, rows_dy = x_ref[...], dy_ref[...]
    for half in range(2):
        cut = slice(half * HALF, (half + 1) * HALF)
        gate_ref[:, cut] = dot(rows_x, packed_ref[half, :, :HALF], ((0,), (0,))).astype(BF16)
        up_ref[:, cut] = dot(rows_x, packed_ref[half, :, HALF : 2 * HALF], ((0,), (0,))).astype(BF16)
        down_ref[cut, :] = dot(packed_ref[half, :, 2 * HALF :], rows_dy, ((0,), (0,))).astype(BF16)


def combine_body(routes_t, returned):
    _, named, rank = slots_of(routes_t)
    place = jnp.bitwise_and(iota((TOK, EXPERTS * 8), 1), 7)
    left = dot(as_bf16(named & (place == 2 * rank)), returned, ((1,), (0,)))
    right = dot(as_bf16(named & (place == 2 * rank + 1)), returned, ((1,), (0,)))
    return jnp.concatenate([left, right], axis=1).astype(BF16)


def combine_kernel(routes_ref, returned_ref, out_ref):
    out_ref[...] = combine_body(routes_ref[...], returned_ref[...])


def call(kernel, outs, flops, *operands):
    shapes = [jax.ShapeDtypeStruct(shape, BF16) for shape in outs]
    moved = sum(x.size * x.dtype.itemsize for x in operands) + sum(2 * s.size for s in shapes)
    return pl.pallas_call(
        kernel,
        out_shape=shapes if len(shapes) > 1 else shapes[0],
        cost_estimate=pl.CostEstimate(flops=flops, bytes_accessed=moved, transcendentals=0),
        compiler_params=pltpu.CompilerParams(vmem_limit_bytes=VMEM_LIMIT),
    )(*operands)


def on_device(acts, grad_out, routes, combine, w_gate, w_up, w_down):
    gate_w, up_w, down_w = w_gate[0], w_up[0], w_down[0]
    slots = EXPERTS * 8
    matmul = 2 * ROWS * WIDTH * HIDDEN

    sent = call(dispatch_kernel, [(slots, WIDTH)], 2 * slots * 144 * WIDTH, routes.T, combine.T, acts, grad_out)
    received = lax.all_to_all(sent.reshape(EXPERTS, 8, WIDTH), "expert", 0, 0, tiled=True)

    parts, rows_x, rows_dy = call(
        product_kernel,
        [(GROUP, 4 * CHUNK, PACK), (ROWS, WIDTH), (ROWS, WIDTH)],
        3 * matmul,
        received.reshape(slots, WIDTH),
        gate_w,
        up_w,
        down_w,
    )
    parts = lax.all_to_all(parts, "dp", 0, 0, tiled=True, axis_index_groups=NEAR)
    parts = call(add_kernel, [(4 * CHUNK, PACK)], 4 * 4 * CHUNK * PACK, parts)
    parts = lax.all_to_all(
        parts.reshape(GROUP, CHUNK, PACK), "dp", 0, 0, tiled=True, axis_index_groups=FAR
    )
    block = call(activate_kernel, [(CHUNK, PACK)], 20 * CHUNK * PACK, parts)
    packed = lax.all_gather(block, "dp", axis=0).reshape(2, ROWS, PACK)

    row_grads = call(row_grad_kernel, [(slots, 128)], 2 * matmul, packed, gate_w, up_w)
    returned = lax.all_to_all(row_grads.reshape(EXPERTS, 8, 128), "expert", 0, 0, tiled=True)
    new_gate, new_up, new_down = call(
        weight_kernel,
        [(WIDTH, HIDDEN), (WIDTH, HIDDEN), (HIDDEN, WIDTH)],
        3 * matmul,
        packed,
        rows_x,
        rows_dy,
    )
    grad_acts = call(
        combine_kernel, [(TOK, WIDTH)], 4 * TOK * slots * 128, routes.T, returned.reshape(slots, 128)
    )
    return grad_acts, new_gate[None], new_up[None], new_down[None]


def solution(mesh):
    return jax.shard_map(
        on_device,
        mesh=mesh,
        in_specs=(
            P("expert", "dp"),
            P("expert", "dp"),
            P("expert", None),
            P("expert", None),
            P("expert", "dp", None),
            P("expert", "dp", None),
            P("expert", None, "dp"),
        ),
        out_specs=(
            P("expert", "dp"),
            P("expert", "dp", None),
            P("expert", "dp", None),
            P("expert", None, "dp"),
        ),
        check_vma=False,
    )
```

time: 278 us -> 144 us (0.52)
  waiting for transfers between devices: 168 us -> 8.83 us
  blocking collectives: 28.2 us -> 111 us
  starting transfers between devices: 48.7 us -> 14.1 us
  between operations: 14.9 us -> 0.68 us
  matrix products: 6.64 us -> 0 us
  local copies, waits for them, and re-layouts: 9.51 us -> 3.77 us
  Pallas kernels: 0 us -> 5.45 us
    unnamed x2 -> x0, waiting for transfers between devices: 142 us -> none
    all_to_all x0 -> x3, blocking collectives: none -> 81.1 us  [the longest x1 29.4 us: on_device(): lax.all_to_all(sent.reshape(EXPERTS, 8, WIDTH), 'expert', 0, 0, tiled=True)]
    all_to_all x3 -> x1, starting transfers between devices: 48.6 us -> 14.1 us  [on_device(): lax.all_to_all(row_grads.reshape(EXPERTS, 8, 128), 'expert', 0, 0, tiled=...]
    all_to_all x3 -> x1, waiting for transfers between devices: 25.9 us -> 8.83 us  [on_device(): lax.all_to_all(row_grads.reshape(EXPERTS, 8, 128), 'expert', 0, 0, tiled=...]
    dot_general x11 -> x0, matrix products: 6.64 us -> none  [the longest x1 1.06 us: on_device(): jnp.einsum('rd,rf->df', rows_x, block_in[:, 1], preferred_element_type=jn...]
    pallas_call x0 -> x7, Pallas kernels: none -> 5.45 us  [call(): pl.pallas_call(kernel, out_shape=shapes if len(shapes) > 1 else shapes[0]...]
  transfers between devices with their start and end apart: 4 -> 1, of which waited for: 4 -> 1; matrix products, arithmetic and copies ran while one was open for 2% -> 0% of each run, Pallas kernels for 0% -> 1%
where the time goes in v1:
time: 144 us
  blocking collectives  111 us (77%)
  starting transfers between devices  14.1 us (10%)
  waiting for transfers between devices  8.83 us (6%)
  Pallas kernels  5.45 us (4%)
  local copies, waits for them, and re-layouts  3.77 us (3%)
    all_gather x1, blocking collectives, on_device(): packed = lax.all_gather(block, 'dp', axis=0).reshape(2, ROWS, PACK)  29.7 us
    all_to_all x1, blocking collectives, on_device(): lax.all_to_all(sent.reshape(EXPERTS, 8, WIDTH), 'expert', 0, 0, tiled=True)  29.4 us
    all_to_all x1, blocking collectives, on_device(): lax.all_to_all(parts.reshape(GROUP, CHUNK, PACK), 'dp', 0, 0, tiled=True,...  27.8 us
    all_to_all x1, blocking collectives, on_device(): lax.all_to_all(parts, 'dp', 0, 0, tiled=True, axis_index_groups=NEAR)  23.9 us
    all_to_all x1, starting transfers between devices, on_device(): lax.all_to_all(row_grads.reshape(EXPERTS, 8, 128), 'expert', 0, 0, tiled=...  14.1 us
    all_to_all x1, waiting for transfers between devices, on_device(): lax.all_to_all(row_grads.reshape(EXPERTS, 8, 128), 'expert', 0, 0, tiled=...  8.83 us
    pallas_call x7, Pallas kernels, call(): pl.pallas_call(kernel, out_shape=shapes if len(shapes) > 1 else shapes[0]...  5.45 us
    unnamed x16, local copies, waits for them, and re-layouts  3.77 us
  transfers between devices with their start and end apart: 1, of which 1 were waited for; matrix products, arithmetic and copies ran while one was open for 0% of the time, Pallas kernels for 1%

profile of v1, /device:TPU:1, one launch (start us, length us, event | category | flops | bytes accessed | tf_op | source)
XLA Modules:
  0.0 143.7 jit_solution(6468867248413122097)
XLA Ops:
  0.6 0.0 copy-start.3
  0.6 0.7 copy-done.3
  1.3 0.0 copy-start.5
  1.3 0.7 copy-done.5
  2.0 0.0 copy-start.6
  2.0 0.7 copy-done.6
  2.7 0.7 copy-done.7
  3.4 0.5 shard_map.102
  3.9 29.4 %all_to_all.20 = bf16[64,8,256]{2,1,0:T(8,128)(2,1)S(1)} all-to-all(bf16[64,8,256]{2,1,0:T(8,128)(2,1)S(1)} %bitcast.20), channel_id=1, replica_groups=mesh['dp'=16,'expert'=64] {'expert'}, dimensions={0} | all-to-all | bytes 524288 | tf_op jit(solution)/shard_map/all_to_all | solution.py:183
  33.4 0.0 copy-done
  33.4 0.0 copy-done.1
  33.4 1.0 copy-done.2
  34.4 0.7 shard_map.103
  35.1 23.9 %all_to_all.21.parts_ref = bf16[4,96,1152]{2,1,0:T(8,128)(2,1)S(1)} all-to-all(bf16[4,96,1152]{2,1,0:T(8,128)(2,1)S(1)} %get-tuple-element.10), channel_id=1, replica_groups={{0,64,128,192},{256,320,384,448},{512,576,640,704},{768,832,896,960},{1..., dimensions={0} | all-to-all | bytes 1769472 | tf_op jit(solution)/shard_map/all_to_all | solution.py:194
  59.0 0.1 shard_map.104
  59.1 27.8 %all_to_all.22.parts_ref = bf16[4,24,1152]{2,1,0:T(8,128)(2,1)S(1)} all-to-all(bf16[4,24,1152]{2,1,0:T(8,128)(2,1)S(1)} %bitcast.22), channel_id=1, replica_groups={{0,256,512,768},{64,320,576,832},{128,384,640,896},{192,448,704,960},{1..., dimensions={0} | all-to-all | bytes 442368 | tf_op jit(solution)/shard_map/all_to_all | solution.py:196
  86.9 29.7 %all-gather = bf16[384,1152]{1,0:T(8,128)(2,1)S(1)} all-gather(bf16[24,1152]{1,0:T(8,128)(2,1)S(1)} %shard_map.105), channel_id=2, replica_groups=mesh['dp'=16,'expert'=64] {'dp'}, dimensions={0}, use_global_device_ids=true | all-gather | bytes 940032 | tf_op jit(solution)/shard_map/all_gather | solution.py:200
  116.7 1.6 %shard_map.106 = bf16[512,128]{1,0:T(8,128)(2,1)} custom-call(bf16[2,192,1152]{2,1,0:T(8,128)(2,1)S(1)} %bitcast.14, bf16[256,768]{1,0:T(8,128)(2,1)S(1)} %bitcast.17, bf16[256,768]{1,0:T(8,128)(2,1)S(1)} %bitcast.19), custom_call_target="tpu_custom_call" | custom-call | flops 150994944 | bytes 1802240 | tf_op jit(solution)/shard_map/pallas_call | solution.py:169
  118.3 14.1 %all-to-all-start.3 = ((bf16[64,8,128]{2,1,0:T(8,128)(2,1)}), bf16[64,8,128]{2,1,0:T(8,128)(2,1)S(1)}, u32[]{:S(2)}, u32[]{:S(2)}) async-start(bf16[64,8,128]{2,1,0:T(8,128)(2,1)} %bitcast.9), calls=%async_computation.3 | async-start | bytes 262144 | tf_op jit(solution)/shard_map/all_to_all | solution.py:203
  132.4 0.0 copy-start.4
  132.4 1.5 %shard_map.108 = (bf16[256,768]{1,0:T(8,128)(2,1)}, bf16[256,768]{1,0:T(8,128)(2,1)}, bf16[768,256]{1,0:T(8,128)(2,1)}) custom-call(bf16[2,192,1152]{2,1,0:T(8,128)(2,1)S(1)} %bitcast.15, bf16[192,256]{1,0:T(8,128)(2,1)S(1)} %get-tuple-element.11.x_ref, bf16[192,256]{1,0:T(8,128)(2,1)S(1)} %get-tuple-element.12.dy_ref), custom_call_target="tpu_custom_call" | custom-call | flops 226492416 | bytes 2260992 | tf_op jit(solution)/shard_map/pallas_call | solution.py:169
  133.9 8.8 %all-to-all-done.3 = bf16[64,8,128]{2,1,0:T(8,128)(2,1)S(1)} async-done(((bf16[64,8,128]{2,1,0:T(8,128)(2,1)}), bf16[64,8,128]{2,1,0:T(8,128)(2,1)S(1)}, u32[]{:S(2)}, u32[]{:S(2)}) %all-to-all-start.3) | async-done | bytes 131104 | tf_op jit(solution)/shard_map/all_to_all | solution.py:203
  142.7 0.0 copy-done.4
  142.7 1.0 shard_map.107
  (5 shorter events, 0.1 us)
Async XLA Ops:
  0.6 0.7 copy-start.3
  1.3 0.7 copy-start.5
  2.0 0.7 copy-start.6
  2.7 0.7 copy-start.7
  3.4 30.0 %copy-start = (bf16[1,256,768]{2,1,0:T(8,128)(2,1)S(1)}, bf16[1,256,768]{2,1,0:T(8,128)(2,1)}, u32[]{:S(2)}) copy-start(bf16[1,256,768]{2,1,0:T(8,128)(2,1)} %param.11) | copy-start | bytes 1179652
  3.4 30.0 %copy-start.1 = (bf16[1,256,768]{2,1,0:T(8,128)(2,1)S(1)}, bf16[1,256,768]{2,1,0:T(8,128)(2,1)}, u32[]{:S(2)}) copy-start(bf16[1,256,768]{2,1,0:T(8,128)(2,1)} %param.12) | copy-start | bytes 1179652
  33.4 1.0 copy-start.2
  118.3 24.5 %all-to-all-start.3 = ((bf16[64,8,128]{2,1,0:T(8,128)(2,1)}), bf16[64,8,128]{2,1,0:T(8,128)(2,1)S(1)}, u32[]{:S(2)}, u32[]{:S(2)}) async-start(bf16[64,8,128]{2,1,0:T(8,128)(2,1)} %bitcast.9), calls=%async_computation.3 | async-start | bytes 262144 | tf_op jit(solution)/shard_map/all_to_all | solution.py:203
  132.4 10.4 %copy-start.4 = (s32[16,8]{0,1:T(8,128)S(1)}, s32[16,8]{0,1:T(8,128)}, u32[]{:S(2)}) copy-start(s32[16,8]{0,1:T(8,128)} %param.9) | copy-start | bytes 1540

commit v2 on v1

v2 whole, which is shorter than its diff:
```python
import functools

import jax
import jax.numpy as jnp
from jax import lax
from jax.experimental import pallas as pl
from jax.experimental.pallas import tpu as pltpu
from jax.sharding import PartitionSpec as P

BF16 = jnp.bfloat16
F32 = jnp.float32
TOK = 16
PICKS = 8
EXPERTS = 64
CAP = 3
ROWS = EXPERTS * CAP
WIDTH = 256
HIDDEN = 768
HALF = HIDDEN // 2
PACK = 3 * HALF
CHUNK = 24
DP = 16
SLOTS = EXPERTS * 8
SAME_PARITY = [[2 * a + b for a in range(DP // 2)] for b in range(2)]
VMEM_LIMIT = 24 * 1024 * 1024


def dot(a, b, contract):
    return lax.dot_general(a, b, (contract, ((), ())), preferred_element_type=F32)


def iota(shape, dim):
    return lax.broadcasted_iota(jnp.int32, shape, dim)


def column(row):
    diagonal = iota((TOK, TOK), 0) == iota((TOK, TOK), 1)
    spread = jnp.where(diagonal, jnp.broadcast_to(row, (TOK, TOK)), jnp.zeros((), row.dtype))
    return jnp.sum(spread, axis=1, keepdims=True)


def slots_of(routes_t):
    expert = lax.shift_right_logical(iota((TOK, SLOTS), 1), 3)
    hits = [column(routes_t[k : k + 1, :]) == expert for k in range(PICKS)]
    named = functools.reduce(jnp.logical_or, hits)
    earlier = (iota((TOK, TOK), 0) > iota((TOK, TOK), 1)).astype(F32).astype(BF16)
    rank = dot(earlier, named.astype(F32).astype(BF16), ((1,), (0,))).astype(jnp.int32)
    return hits, named, rank


def as_bf16(mask):
    return mask.astype(F32).astype(BF16)


def dispatch_body(routes_t, combine_t, acts, grad_out):
    hits, named, rank = slots_of(routes_t)
    place = jnp.bitwise_and(iota((TOK, SLOTS), 1), 7)
    wanted_x = place == rank
    wanted_dy = place == rank + 4
    choose = [as_bf16(named & wanted_x)] + [as_bf16(hit & wanted_dy) for hit in hits]
    wide = grad_out.astype(F32)
    values = [acts] + [(column(combine_t[k : k + 1, :]) * wide).astype(BF16) for k in range(PICKS)]
    sent = dot(jnp.concatenate(choose, axis=0), jnp.concatenate(values, axis=0), ((0,), (0,)))
    back = [as_bf16(named & (place == 2 * rank + half)) for half in range(2)]
    return sent.astype(BF16), jnp.concatenate(back, axis=0)


def dispatch_kernel(routes, combine, acts, grad_out, sent_ref, back_ref, *scratch):
    held, arrived = scratch[:4], scratch[4]
    copies = [
        pltpu.make_async_copy(source, place, arrived.at[i])
        for i, (source, place) in enumerate(zip((routes, combine, acts, grad_out), held))
    ]
    for copy in copies:
        copy.start()
    for copy in copies:
        copy.wait()
    sent_ref[...], back_ref[...] = dispatch_body(*(place[...] for place in held))


def take_rows(received, row):
    base = jnp.bitwise_and(row, EXPERTS - 1) * 8 + lax.shift_right_logical(row, 6)
    slot = iota((ROWS, SLOTS), 1)
    rows_x = dot(as_bf16(slot == base), received, ((1,), (0,))).astype(BF16)
    rows_dy = dot(as_bf16(slot == base + 4), received, ((1,), (0,))).astype(BF16)
    return rows_x, rows_dy


def own_rows_first(parity):
    place = iota((ROWS, 1), 0)
    second = (place >= ROWS // 2).astype(jnp.int32)
    within = place - second * (ROWS // 2)
    chunk = sum((within >= CHUNK * i).astype(jnp.int32) for i in range(1, 4))
    return within + CHUNK * chunk + CHUNK * jnp.bitwise_xor(second, parity)


def products(rows_x, rows_dy, w_gate, w_up, w_down):
    gate = dot(rows_x, w_gate, ((1,), (0,)))
    up = dot(rows_x, w_up, ((1,), (0,)))
    back = dot(rows_dy, w_down(), ((1,), (1,)))
    cuts = [slice(half * HALF, (half + 1) * HALF) for half in range(2)]
    return [jnp.concatenate([gate[:, cut], up[:, cut], back[:, cut]], axis=1) for cut in cuts]


def product_kernel(received_ref, w_gate_ref, w_up_ref, w_down, own_ref, send_ref, down_ref, arrived):
    copy = pltpu.make_async_copy(w_down, down_ref, arrived)
    copy.start()

    def held():
        copy.wait()
        return down_ref[...]

    parity = jnp.bitwise_and(lax.axis_index("dp"), 1)
    rows_x, rows_dy = take_rows(received_ref[...], own_rows_first(parity))
    halves = products(rows_x, rows_dy, w_gate_ref[...], w_up_ref[...], held)
    for half, both in enumerate(halves):
        own_ref[half] = both[: ROWS // 2]
        send_ref[half] = both[ROWS // 2 :].astype(BF16)


def pair_body(own, taken):
    return (own + taken.astype(F32)).astype(BF16)


def pair_kernel(own_ref, taken_ref, out_ref):
    out_ref[...] = pair_body(own_ref[...], taken_ref[...])


def activate_body(parts):
    total = [parts[i].astype(F32) for i in range(8)]
    while len(total) > 1:
        total = [total[i] + total[i + 1] for i in range(0, len(total), 2)]
    total = total[0]
    pre_gate, pre_up, hidden_grad = total[:, :HALF], total[:, HALF : 2 * HALF], total[:, 2 * HALF :]
    sigmoid_gate = jax.nn.sigmoid(pre_gate)
    silu_gate = pre_gate * sigmoid_gate
    hidden = silu_gate * pre_up
    up_grad = hidden_grad * silu_gate
    gate_grad = hidden_grad * pre_up * sigmoid_gate * (1.0 + pre_gate * (1.0 - sigmoid_gate))
    return jnp.concatenate([gate_grad, up_grad, hidden], axis=1).astype(BF16)


def activate_kernel(parts_ref, out_ref):
    out_ref[...] = activate_body(parts_ref[...])


def row_grad_body(packed, w_gate, w_up):
    total = jnp.zeros((ROWS, WIDTH), F32)
    for half in range(2):
        cut = slice(half * HALF, (half + 1) * HALF)
        total += dot(packed[half][:, :HALF], w_gate[:, cut], ((1,), (1,)))
        total += dot(packed[half][:, HALF : 2 * HALF], w_up[:, cut], ((1,), (1,)))
    rounded = total.astype(BF16)
    slot, row = iota((SLOTS, ROWS), 0), iota((1, ROWS), 1)
    base = jnp.bitwise_and(row, EXPERTS - 1) * 8 + lax.shift_right_logical(row, 6) * 2
    left = dot(as_bf16(slot == base), rounded[:, :128], ((1,), (0,)))
    right = dot(as_bf16(slot == base + 1), rounded[:, 128:], ((1,), (0,)))
    return (left + right).astype(BF16)


def row_grad_kernel(packed_ref, w_gate_ref, w_up_ref, out_ref):
    out_ref[...] = row_grad_body(packed_ref[...], w_gate_ref[...], w_up_ref[...])


def weight_kernel(packed_ref, received_ref, gate_ref, up_ref, down_ref):
    rows_x, rows_dy = take_rows(received_ref[...], iota((ROWS, 1), 0))
    for half in range(2):
        cut = slice(half * HALF, (half + 1) * HALF)
        gate_ref[:, cut] = dot(rows_x, packed_ref[half, :, :HALF], ((0,), (0,))).astype(BF16)
        up_ref[:, cut] = dot(rows_x, packed_ref[half, :, HALF : 2 * HALF], ((0,), (0,))).astype(BF16)
        down_ref[cut, :] = dot(packed_ref[half, :, 2 * HALF :], rows_dy, ((0,), (0,))).astype(BF16)


def combine_body(back, returned):
    left = dot(back[:TOK], returned, ((1,), (0,)))
    right = dot(back[TOK:], returned, ((1,), (0,)))
    return jnp.concatenate([left, right], axis=1).astype(BF16)


def combine_kernel(back_ref, returned_ref, out_ref):
    out_ref[...] = combine_body(back_ref[...], returned_ref[...])


def call(kernel, outs, flops, *operands, **options):
    shapes = [jax.ShapeDtypeStruct(shape, dtype) for shape, dtype in outs]
    moved = sum(x.size * x.dtype.itemsize for x in [*operands, *shapes])
    return pl.pallas_call(
        kernel,
        out_shape=shapes if len(shapes) > 1 else shapes[0],
        cost_estimate=pl.CostEstimate(flops=flops, bytes_accessed=moved, transcendentals=0),
        compiler_params=pltpu.CompilerParams(vmem_limit_bytes=VMEM_LIMIT),
        **options,
    )(*operands)


ANY = pl.BlockSpec(memory_space=pl.ANY)
VMEM = pl.BlockSpec(memory_space=pltpu.VMEM)


def on_device(acts, grad_out, routes, combine, w_gate, w_up, w_down):
    gate_w, up_w, down_w = w_gate[0], w_up[0], w_down[0]
    matmul = 2 * ROWS * WIDTH * HIDDEN

    sent, back = call(
        dispatch_kernel,
        [((SLOTS, WIDTH), BF16), ((2 * TOK, SLOTS), BF16)],
        2 * SLOTS * 144 * WIDTH,
        routes.T,
        combine.T,
        acts,
        grad_out,
        in_specs=[ANY] * 4,
        scratch_shapes=[
            pltpu.VMEM((PICKS, TOK), jnp.int32),
            pltpu.VMEM((PICKS, TOK), F32),
            pltpu.VMEM((TOK, WIDTH), BF16),
            pltpu.VMEM((TOK, WIDTH), BF16),
            pltpu.SemaphoreType.DMA((4,)),
        ],
    )
    received = lax.all_to_all(sent.reshape(EXPERTS, 8, WIDTH), "expert", 0, 0, tiled=True)
    received = received.reshape(SLOTS, WIDTH)

    own, send = call(
        product_kernel,
        [((2, ROWS // 2, PACK), F32), ((2, ROWS // 2, PACK), BF16)],
        3 * matmul,
        received,
        gate_w,
        up_w,
        down_w,
        in_specs=[VMEM, VMEM, VMEM, ANY],
        scratch_shapes=[pltpu.VMEM((HIDDEN, WIDTH), BF16), pltpu.SemaphoreType.DMA(())],
    )
    taken = lax.ppermute(send, "dp", [(i, i ^ 1) for i in range(DP)])
    parts = call(pair_kernel, [((2, ROWS // 2, PACK), BF16)], ROWS * PACK, own, taken)
    parts = lax.all_to_all(
        parts.reshape(DP // 2, CHUNK, PACK), "dp", 0, 0, tiled=True, axis_index_groups=SAME_PARITY
    )
    block = call(activate_kernel, [((CHUNK, PACK), BF16)], 20 * CHUNK * PACK, parts)
    packed = lax.all_gather(block, "dp", axis=0).reshape(2, ROWS, PACK)

    row_grads = call(row_grad_kernel, [((SLOTS, 128), BF16)], 2 * matmul, packed, gate_w, up_w)
    returned = lax.all_to_all(row_grads.reshape(EXPERTS, 8, 128), "expert", 0, 0, tiled=True)
    new_gate, new_up, new_down = call(
        weight_kernel,
        [((WIDTH, HIDDEN), BF16), ((WIDTH, HIDDEN), BF16), ((HIDDEN, WIDTH), BF16)],
        3 * matmul,
        packed,
        received,
    )
    grad_acts = call(
        combine_kernel, [((TOK, WIDTH), BF16)], 4 * TOK * SLOTS * 128, back, returned.reshape(SLOTS, 128)
    )
    return grad_acts, new_gate[None], new_up[None], new_down[None]


def solution(mesh):
    return jax.shard_map(
        on_device,
        mesh=mesh,
        in_specs=(
            P("expert", "dp"),
            P("expert", "dp"),
            P("expert", None),
            P("expert", None),
            P("expert", "dp", None),
            P("expert", "dp", None),
            P("expert", None, "dp"),
        ),
        out_specs=(
            P("expert", "dp"),
            P("expert", "dp", None),
            P("expert", "dp", None),
            P("expert", None, "dp"),
        ),
        check_vma=False,
    )
```

time: 144 us -> 143 us (level)
  blocking collectives: 111 us -> 95.2 us
  waiting for transfers between devices: 8.83 us -> 19.7 us
  starting transfers between devices: 14.1 us -> 16.3 us
    all_to_all x2 -> x1, blocking collectives: 51.7 us -> 33 us  [on_device(): lax.all_to_all(parts.reshape(DP // 2, CHUNK, PACK), 'dp', 0, 0, tiled=Tru...]
    ppermute x0 -> x1, waiting for transfers between devices: none -> 11.2 us  [on_device(): taken = lax.ppermute(send, 'dp', [(i, i ^ 1) for i in range(DP)])]
    all_gather x1, blocking collectives: 29.7 us -> 32.8 us  [on_device(): packed = lax.all_gather(block, 'dp', axis=0).reshape(2, ROWS, PACK)]
    ppermute x0 -> x1, starting transfers between devices: none -> 1.92 us  [on_device(): taken = lax.ppermute(send, 'dp', [(i, i ^ 1) for i in range(DP)])]
  transfers between devices with their start and end apart: 1 -> 2, of which waited for: 1 -> 2; matrix products, arithmetic and copies ran while one was open for 0% -> 0% of each run, Pallas kernels for 1% -> 1%
where the time goes in v2:
time: 143 us
  blocking collectives  95.2 us (67%)
  waiting for transfers between devices  19.7 us (14%)
  starting transfers between devices  16.3 us (11%)
  Pallas kernels  5.97 us (4%)
  local copies, waits for them, and re-layouts  4.81 us (3%)
    all_to_all x1, blocking collectives, on_device(): lax.all_to_all(parts.reshape(DP // 2, CHUNK, PACK), 'dp', 0, 0, tiled=Tru...  33 us
    all_gather x1, blocking collectives, on_device(): packed = lax.all_gather(block, 'dp', axis=0).reshape(2, ROWS, PACK)  32.8 us
    all_to_all x1, blocking collectives, on_device(): lax.all_to_all(sent.reshape(EXPERTS, 8, WIDTH), 'expert', 0, 0, tiled=True)  29.4 us
    all_to_all x1, starting transfers between devices, on_device(): lax.all_to_all(row_grads.reshape(EXPERTS, 8, 128), 'expert', 0, 0, tiled=...  14.4 us
    ppermute x1, waiting for transfers between devices, on_device(): taken = lax.ppermute(send, 'dp', [(i, i ^ 1) for i in range(DP)])  11.2 us
    all_to_all x1, waiting for transfers between devices, on_device(): lax.all_to_all(row_grads.reshape(EXPERTS, 8, 128), 'expert', 0, 0, tiled=...  8.58 us
    pallas_call x7, Pallas kernels, call(): pl.pallas_call(kernel, out_shape=shapes if len(shapes) > 1 else shapes[0]...  5.97 us
    unnamed x16, local copies, waits for them, and re-layouts  4.81 us
  transfers between devices with their start and end apart: 2, of which 2 were waited for; matrix products, arithmetic and copies ran while one was open for 0% of the time, Pallas kernels for 1%

profile of v2, /device:TPU:1, one launch (start us, length us, event | category | flops | bytes accessed | tf_op | source)
XLA Modules:
  0.0 142.7 jit_solution(4891922426023465502)
XLA Ops:
  0.6 0.0 copy-start
  0.7 0.7 copy-done.4
  1.4 0.7 copy-done.5
  2.1 0.7 copy-done.6
  2.8 0.7 copy-done.7
  3.5 0.6 shard_map.102
  4.1 29.4 %all_to_all.15 = bf16[64,8,256]{2,1,0:T(8,128)(2,1)S(1)} all-to-all(bf16[64,8,256]{2,1,0:T(8,128)(2,1)S(1)} %bitcast.25), channel_id=1, replica_groups=mesh['dp'=16,'expert'=64] {'expert'}, dimensions={0} | all-to-all | bytes 524288 | tf_op jit(solution)/shard_map/all_to_all | solution.py:221
  33.5 0.0 copy-done
  33.5 1.0 copy-done.1
  34.5 1.0 copy-done.3
  35.5 1.1 shard_map.103
  36.6 1.9 %collective-permute-start = (bf16[2,96,1152]{2,1,0:T(8,128)(2,1)S(1)}, bf16[2,96,1152]{2,1,0:T(8,128)(2,1)S(1)}, u32[]{:S(2)}, u32[]{:S(2)}) collective-permute-start(bf16[2,96,1152]{2,1,0:T(8,128)(2,1)S(1)} %get-tuple-element.14), channel_id=1, source_target_pairs={{0,64},{64,0},{128,192},{192,128},{256,320},{320,256},{384,448},{4... | collective-permute-start | bytes 1327112 | tf_op jit(solution)/shard_map/ppermute | solution.py:235
  38.5 11.2 %collective-permute-done.taken_ref = bf16[2,96,1152]{2,1,0:T(8,128)(2,1)S(1)} collective-permute-done((bf16[2,96,1152]{2,1,0:T(8,128)(2,1)S(1)}, bf16[2,96,1152]{2,1,0:T(8,128)(2,1)S(1)}, u32[]{:S(2)}, u32[]{:S(2)}) %collective-permute-start) | collective-permute-done | bytes 442400 | tf_op jit(solution)/shard_map/ppermute | solution.py:235
  49.7 0.1 shard_map.104
  49.7 33.0 %all_to_all.16.parts_ref = bf16[8,24,1152]{2,1,0:T(8,128)(2,1)S(1)} all-to-all(bf16[8,24,1152]{2,1,0:T(8,128)(2,1)S(1)} %bitcast.18), channel_id=1, replica_groups={{0,128,256,384,512,640,768,896},{64,192,320,448,576,704,832,960},{1,129..., dimensions={0} | all-to-all | bytes 884736 | tf_op jit(solution)/shard_map/all_to_all | solution.py:237
  82.8 0.1 shard_map.105
  82.8 0.0 copy-start.2
  82.9 32.8 %all-gather = bf16[384,1152]{1,0:T(8,128)(2,1)S(1)} all-gather(bf16[24,1152]{1,0:T(8,128)(2,1)S(1)} %shard_map.105), channel_id=2, replica_groups=mesh['dp'=16,'expert'=64] {'dp'}, dimensions={0}, use_global_device_ids=true | all-gather | bytes 940032 | tf_op jit(solution)/shard_map/all_gather | solution.py:241
  115.6 0.0 copy-done.2
  115.6 1.6 %shard_map.106 = bf16[512,128]{1,0:T(8,128)(2,1)} custom-call(bf16[2,192,1152]{2,1,0:T(8,128)(2,1)S(1)} %bitcast.14, bf16[256,768]{1,0:T(8,128)(2,1)S(1)} %bitcast.20, bf16[256,768]{1,0:T(8,128)(2,1)S(1)} %bitcast.22), custom_call_target="tpu_custom_call" | custom-call | flops 150994944 | bytes 1802240 | tf_op jit(solution)/shard_map/pallas_call | solution.py:187
  117.2 14.4 %all-to-all-start.2 = ((bf16[64,8,128]{2,1,0:T(8,128)(2,1)}), bf16[64,8,128]{2,1,0:T(8,128)(2,1)S(1)}, u32[]{:S(2)}, u32[]{:S(2)}) async-start(bf16[64,8,128]{2,1,0:T(8,128)(2,1)} %bitcast.9), calls=%async_computation.2 | async-start | bytes 262144 | tf_op jit(solution)/shard_map/all_to_all | solution.py:244
  131.6 1.8 %shard_map.108 = (bf16[256,768]{1,0:T(8,128)(2,1)}, bf16[256,768]{1,0:T(8,128)(2,1)}, bf16[768,256]{1,0:T(8,128)(2,1)}) custom-call(bf16[2,192,1152]{2,1,0:T(8,128)(2,1)S(1)} %bitcast.15, bf16[512,256]{1,0:T(8,128)(2,1)S(1)} %bitcast.17), custom_call_target="tpu_custom_call" | custom-call | flops 226492416 | bytes 2326528 | tf_op jit(solution)/shard_map/pallas_call | solution.py:187
  133.4 8.6 %all-to-all-done.2 = bf16[64,8,128]{2,1,0:T(8,128)(2,1)S(1)} async-done(((bf16[64,8,128]{2,1,0:T(8,128)(2,1)}), bf16[64,8,128]{2,1,0:T(8,128)(2,1)S(1)}, u32[]{:S(2)}, u32[]{:S(2)}) %all-to-all-start.2) | async-done | bytes 131104 | tf_op jit(solution)/shard_map/all_to_all | solution.py:244
  141.9 0.8 shard_map.107
  (6 shorter events, 0.0 us)
Async XLA Ops:
  0.6 32.8 %copy-start = (bf16[1,256,768]{2,1,0:T(8,128)(2,1)S(1)}, bf16[1,256,768]{2,1,0:T(8,128)(2,1)}, u32[]{:S(2)}) copy-start(bf16[1,256,768]{2,1,0:T(8,128)(2,1)} %param.11) | copy-start | bytes 1179652
  0.6 0.7 copy-start.4
  1.4 0.7 copy-start.5
  2.1 0.7 copy-start.6
  2.8 0.7 copy-start.7
  33.5 1.0 copy-start.1
  34.5 1.0 copy-start.3
  36.6 13.1 %collective-permute-start = (bf16[2,96,1152]{2,1,0:T(8,128)(2,1)S(1)}, bf16[2,96,1152]{2,1,0:T(8,128)(2,1)S(1)}, u32[]{:S(2)}, u32[]{:S(2)}) collective-permute-start(bf16[2,96,1152]{2,1,0:T(8,128)(2,1)S(1)} %get-tuple-element.14), channel_id=1, source_target_pairs={{0,64},{64,0},{128,192},{192,128},{256,320},{320,256},{384,448},{4... | collective-permute-start | bytes 1327112 | tf_op jit(solution)/shard_map/ppermute | solution.py:235
  82.8 32.8 %copy-start.2 = (bf16[1,256,768]{2,1,0:T(8,128)(2,1)S(1)}, bf16[1,256,768]{2,1,0:T(8,128)(2,1)}, u32[]{:S(2)}) copy-start(bf16[1,256,768]{2,1,0:T(8,128)(2,1)} %param.12) | copy-start | bytes 1179652
  117.2 24.7 %all-to-all-start.2 = ((bf16[64,8,128]{2,1,0:T(8,128)(2,1)}), bf16[64,8,128]{2,1,0:T(8,128)(2,1)S(1)}, u32[]{:S(2)}, u32[]{:S(2)}) async-start(bf16[64,8,128]{2,1,0:T(8,128)(2,1)} %bitcast.9), calls=%async_computation.2 | async-start | bytes 262144 | tf_op jit(solution)/shard_map/all_to_all | solution.py:244

commit v3 on v2

--- a/solution.py
+++ b/solution.py
@@ -22,6 +22,15 @@
 DP = 16
 SLOTS = EXPERTS * 8
 SAME_PARITY = [[2 * a + b for a in range(DP // 2)] for b in range(2)]
+def partner(dp, expert):
+    if expert % 2 == 0:
+        return dp ^ 1
+    return (dp + 1) % DP if dp % 2 else (dp - 1) % DP
+
+
+PAIRS = [
+    (dp * EXPERTS + expert, partner(dp, expert) * EXPERTS + expert) for dp in range(DP) for expert in range(EXPERTS)
+]
 VMEM_LIMIT = 24 * 1024 * 1024
 
 
@@ -78,59 +87,54 @@
     sent_ref[...], back_ref[...] = dispatch_body(*(place[...] for place in held))
 
 
-def take_rows(received, row):
-    base = jnp.bitwise_and(row, EXPERTS - 1) * 8 + lax.shift_right_logical(row, 6)
-    slot = iota((ROWS, SLOTS), 1)
-    rows_x = dot(as_bf16(slot == base), received, ((1,), (0,))).astype(BF16)
-    rows_dy = dot(as_bf16(slot == base + 4), received, ((1,), (0,))).astype(BF16)
-    return rows_x, rows_dy
-
-
-def own_rows_first(parity):
-    place = iota((ROWS, 1), 0)
-    second = (place >= ROWS // 2).astype(jnp.int32)
-    within = place - second * (ROWS // 2)
-    chunk = sum((within >= CHUNK * i).astype(jnp.int32) for i in range(1, 4))
-    return within + CHUNK * chunk + CHUNK * jnp.bitwise_xor(second, parity)
+def take_rows(received_ref, held):
+    parts = []
+    for half in range(2):
+        held[half] = received_ref[:, 128 * half : 128 * (half + 1)].astype(F32)
+        parts.append([held[half, pl.Slice(place, EXPERTS, 8), :] for place in range(7)])
+    full = [jnp.concatenate(pair, axis=1).astype(BF16) for pair in zip(*parts)]
+    return jnp.concatenate(full[:CAP], axis=0), jnp.concatenate(full[4 : 4 + CAP], axis=0)
 
 
 def products(rows_x, rows_dy, w_gate, w_up, w_down):
     gate = dot(rows_x, w_gate, ((1,), (0,)))
     up = dot(rows_x, w_up, ((1,), (0,)))
-    back = dot(rows_dy, w_down(), ((1,), (1,)))
+    back = dot(rows_dy, w_down, ((1,), (1,)))
     cuts = [slice(half * HALF, (half + 1) * HALF) for half in range(2)]
     return [jnp.concatenate([gate[:, cut], up[:, cut], back[:, cut]], axis=1) for cut in cuts]
 
 
-def product_kernel(received_ref, w_gate_ref, w_up_ref, w_down, own_ref, send_ref, down_ref, arrived):
-    copy = pltpu.make_async_copy(w_down, down_ref, arrived)
-    copy.start()
-
-    def held():
-        copy.wait()
-        return down_ref[...]
-
+def split_rows(both, parity):
+    even, odd = (
+        jnp.concatenate([both[CHUNK * i : CHUNK * (i + 1)] for i in range(first, 8, 2)], axis=0)
+        for first in range(2)
+    )
+    is_odd = parity == 1
+    return jnp.where(is_odd, odd, even), jnp.where(is_odd, even, odd)
+
+
+def product_kernel(received_ref, w_gate_ref, w_up_ref, w_down_ref, own_ref, send_ref, held):
+    rows_x, rows_dy = take_rows(received_ref, held)
     parity = jnp.bitwise_and(lax.axis_index("dp"), 1)
-    rows_x, rows_dy = take_rows(received_ref[...], own_rows_first(parity))
-    halves = products(rows_x, rows_dy, w_gate_ref[...], w_up_ref[...], held)
-    for half, both in enumerate(halves):
-        own_ref[half] = both[: ROWS // 2]
-        send_ref[half] = both[ROWS // 2 :].astype(BF16)
-
-
-def pair_body(own, taken):
-    return (own + taken.astype(F32)).astype(BF16)
-
-
-def pair_kernel(own_ref, taken_ref, out_ref):
-    out_ref[...] = pair_body(own_ref[...], taken_ref[...])
-
-
-def activate_body(parts):
+    for half, both in enumerate(products(rows_x, rows_dy, w_gate_ref[...], w_up_ref[...], w_down_ref[...])):
+        own, other = split_rows(both, parity)
+        own_ref[half] = own
+        send_ref[half] = other.astype(BF16)
+
+
+def pair_kernel(own_ref, taken_ref, out_ref, left_ref):
+    total = own_ref[...] + taken_ref[...].astype(F32)
+    out_ref[...] = total.astype(BF16)
+    mine = lax.shift_right_logical(lax.axis_index("dp"), 1)
+    kept = own_ref[mine] + taken_ref[mine].astype(F32)
+    left_ref[...] = kept - kept.astype(BF16).astype(F32)
+
+
+def activate_body(parts, left):
     total = [parts[i].astype(F32) for i in range(8)]
     while len(total) > 1:
         total = [total[i] + total[i + 1] for i in range(0, len(total), 2)]
-    total = total[0]
+    total = total[0] + left
     pre_gate, pre_up, hidden_grad = total[:, :HALF], total[:, HALF : 2 * HALF], total[:, 2 * HALF :]
     sigmoid_gate = jax.nn.sigmoid(pre_gate)
     silu_gate = pre_gate * sigmoid_gate
@@ -140,8 +144,8 @@
     return jnp.concatenate([gate_grad, up_grad, hidden], axis=1).astype(BF16)
 
 
-def activate_kernel(parts_ref, out_ref):
-    out_ref[...] = activate_body(parts_ref[...])
+def activate_kernel(parts_ref, left_ref, out_ref):
+    out_ref[...] = activate_body(parts_ref[...], left_ref[...])
 
 
 def row_grad_body(packed, w_gate, w_up):
@@ -150,20 +154,23 @@
         cut = slice(half * HALF, (half + 1) * HALF)
         total += dot(packed[half][:, :HALF], w_gate[:, cut], ((1,), (1,)))
         total += dot(packed[half][:, HALF : 2 * HALF], w_up[:, cut], ((1,), (1,)))
-    rounded = total.astype(BF16)
-    slot, row = iota((SLOTS, ROWS), 0), iota((1, ROWS), 1)
-    base = jnp.bitwise_and(row, EXPERTS - 1) * 8 + lax.shift_right_logical(row, 6) * 2
-    left = dot(as_bf16(slot == base), rounded[:, :128], ((1,), (0,)))
-    right = dot(as_bf16(slot == base + 1), rounded[:, 128:], ((1,), (0,)))
-    return (left + right).astype(BF16)
-
-
-def row_grad_kernel(packed_ref, w_gate_ref, w_up_ref, out_ref):
-    out_ref[...] = row_grad_body(packed_ref[...], w_gate_ref[...], w_up_ref[...])
-
-
-def weight_kernel(packed_ref, received_ref, gate_ref, up_ref, down_ref):
-    rows_x, rows_dy = take_rows(received_ref[...], iota((ROWS, 1), 0))
+    return total
+
+
+def row_grad_kernel(packed_ref, w_gate_ref, w_up_ref, out_ref, held):
+    total = row_grad_body(packed_ref[...], w_gate_ref[...], w_up_ref[...])
+    for place in range(8):
+        slot, half = divmod(place, 2)
+        if slot < CAP:
+            value = total[EXPERTS * slot : EXPERTS * (slot + 1), 128 * half : 128 * (half + 1)]
+        else:
+            value = jnp.zeros((EXPERTS, 128), F32)
+        held[pl.Slice(place, EXPERTS, 8), :] = value
+    out_ref[...] = held[...].astype(BF16)
+
+
+def weight_kernel(packed_ref, received_ref, gate_ref, up_ref, down_ref, held):
+    rows_x, rows_dy = take_rows(received_ref, held)
     for half in range(2):
         cut = slice(half * HALF, (half + 1) * HALF)
         gate_ref[:, cut] = dot(rows_x, packed_ref[half, :, :HALF], ((0,), (0,))).astype(BF16)
@@ -193,8 +200,8 @@
     )(*operands)
 
 
-ANY = pl.BlockSpec(memory_space=pl.ANY)
-VMEM = pl.BlockSpec(memory_space=pltpu.VMEM)
+HBM = pl.BlockSpec(memory_space=pltpu.HBM)
+TAKEN = pltpu.VMEM((2, SLOTS, 128), F32)
 
 
 def on_device(acts, grad_out, routes, combine, w_gate, w_up, w_down):
@@ -204,12 +211,9 @@
     sent, back = call(
         dispatch_kernel,
         [((SLOTS, WIDTH), BF16), ((2 * TOK, SLOTS), BF16)],
-        2 * SLOTS * 144 * WIDTH,
-        routes.T,
-        combine.T,
-        acts,
-        grad_out,
-        in_specs=[ANY] * 4,
+        4 * matmul,
+        *(pltpu.with_memory_space_constraint(x, pltpu.HBM) for x in (routes.T, combine.T, acts, grad_out)),
+        in_specs=[HBM] * 4,
         scratch_shapes=[
             pltpu.VMEM((PICKS, TOK), jnp.int32),
             pltpu.VMEM((PICKS, TOK), F32),
@@ -229,18 +233,22 @@
         gate_w,
         up_w,
         down_w,
-        in_specs=[VMEM, VMEM, VMEM, ANY],
-        scratch_shapes=[pltpu.VMEM((HIDDEN, WIDTH), BF16), pltpu.SemaphoreType.DMA(())],
-    )
-    taken = lax.ppermute(send, "dp", [(i, i ^ 1) for i in range(DP)])
-    parts = call(pair_kernel, [((2, ROWS // 2, PACK), BF16)], ROWS * PACK, own, taken)
-    parts = lax.all_to_all(
-        parts.reshape(DP // 2, CHUNK, PACK), "dp", 0, 0, tiled=True, axis_index_groups=SAME_PARITY
-    )
-    block = call(activate_kernel, [((CHUNK, PACK), BF16)], 20 * CHUNK * PACK, parts)
+        scratch_shapes=[TAKEN],
+    )
+    taken = lax.ppermute(send, ("dp", "expert"), PAIRS)
+    eighths = (DP // 2, CHUNK, PACK)
+    parts, left = call(
+        pair_kernel,
+        [(eighths, BF16), ((CHUNK, PACK), F32)],
+        ROWS * PACK,
+        own.reshape(eighths),
+        taken.reshape(eighths),
+    )
+    parts = lax.all_to_all(parts, "dp", 0, 0, tiled=True, axis_index_groups=SAME_PARITY)
+    block = call(activate_kernel, [((CHUNK, PACK), BF16)], 20 * CHUNK * PACK, parts, left)
     packed = lax.all_gather(block, "dp", axis=0).reshape(2, ROWS, PACK)
 
-    row_grads = call(row_grad_kernel, [((SLOTS, 128), BF16)], 2 * matmul, packed, gate_w, up_w)
+    row_grads = call(row_grad_kernel, [((SLOTS, 128), BF16)], 2 * matmul, packed, gate_w, up_w, scratch_shapes=[pltpu.VMEM((SLOTS, 128), F32)])
     returned = lax.all_to_all(row_grads.reshape(EXPERTS, 8, 128), "expert", 0, 0, tiled=True)
     new_gate, new_up, new_down = call(
         weight_kernel,
@@ -248,6 +256,7 @@
         3 * matmul,
         packed,
         received,
+        scratch_shapes=[TAKEN],
     )
     grad_acts = call(
         combine_kernel, [((TOK, WIDTH), BF16)], 4 * TOK * SLOTS * 128, back, returned.reshape(SLOTS, 128)

time: 143 us -> 136 us (0.951)
  starting transfers between devices: 16.3 us -> 26.7 us
  blocking collectives: 95.2 us -> 88 us
  waiting for transfers between devices: 19.7 us -> 14.5 us
  local copies, waits for them, and re-layouts: 4.81 us -> 0.01 us
    ppermute x1, starting transfers between devices: 1.92 us -> 11.9 us  [on_device(): taken = lax.ppermute(send, ('dp', 'expert'), PAIRS)]
    ppermute x1, waiting for transfers between devices: 11.2 us -> 5.68 us  [on_device(): taken = lax.ppermute(send, ('dp', 'expert'), PAIRS)]
    unnamed x16 -> x6, local copies, waits for them, and re-layouts: 4.81 us -> 0.01 us
    all_to_all x1, blocking collectives: 33 us -> 28.8 us  [on_device(): lax.all_to_all(parts, 'dp', 0, 0, tiled=True, axis_index_groups=SAME_PARITY)]
    all_gather x1, blocking collectives: 32.8 us -> 29.6 us  [on_device(): packed = lax.all_gather(block, 'dp', axis=0).reshape(2, ROWS, PACK)]
where the time goes in v3:
time: 136 us; the launch traced here: 135 us
  blocking collectives  88 us (65%)
  starting transfers between devices  26.7 us (20%)
  waiting for transfers between devices  14.5 us (11%)
  Pallas kernels  5.48 us (4%)
    all_gather x1, blocking collectives, on_device(): packed = lax.all_gather(block, 'dp', axis=0).reshape(2, ROWS, PACK)  29.6 us
    all_to_all x1, blocking collectives, on_device(): lax.all_to_all(sent.reshape(EXPERTS, 8, WIDTH), 'expert', 0, 0, tiled=True)  29.6 us
    all_to_all x1, blocking collectives, on_device(): lax.all_to_all(parts, 'dp', 0, 0, tiled=True, axis_index_groups=SAME_PARITY)  28.8 us
    all_to_all x1, starting transfers between devices, on_device(): lax.all_to_all(row_grads.reshape(EXPERTS, 8, 128), 'expert', 0, 0, tiled=...  14.7 us
    ppermute x1, starting transfers between devices, on_device(): taken = lax.ppermute(send, ('dp', 'expert'), PAIRS)  11.9 us
    all_to_all x1, waiting for transfers between devices, on_device(): lax.all_to_all(row_grads.reshape(EXPERTS, 8, 128), 'expert', 0, 0, tiled=...  8.79 us
    ppermute x1, waiting for transfers between devices, on_device(): taken = lax.ppermute(send, ('dp', 'expert'), PAIRS)  5.68 us
    pallas_call x7, Pallas kernels, call(): pl.pallas_call(kernel, out_shape=shapes if len(shapes) > 1 else shapes[0]...  5.48 us
  transfers between devices with their start and end apart: 2, of which 2 were waited for; matrix products, arithmetic and copies ran while one was open for 0% of the time, Pallas kernels for 1%

profile of v3, /device:TPU:1, one launch (start us, length us, event | category | flops | bytes accessed | tf_op | source)
XLA Modules:
  0.0 135.3 jit_solution(4430782537110950684)
XLA Ops:
  0.6 0.0 copy-start.1
  0.6 0.0 copy-start.2
  0.7 1.4 %shard_map.102 = (bf16[512,256]{1,0:T(8,128)(2,1)S(1)}, bf16[32,512]{1,0:T(8,128)(2,1)S(1)}) custom-call(s32[8,16]{1,0:T(8,128)} %bitcast.31, f32[8,16]{1,0:T(8,128)} %bitcast.32, bf16[16,256]{1,0:T(8,128)(2,1)} %acts.1, bf16[16,256]{1,0:T(8,128)(2,1)} %grad_out.1), custom_call_target="tpu_custom_call" | custom-call | flops 301989888 | bytes 312320 | tf_op jit(solution)/shard_map/pallas_call | solution.py:194
  2.0 0.0 copy-start
  2.1 29.6 %all_to_all.15 = bf16[64,8,256]{2,1,0:T(8,128)(2,1)S(1)} all-to-all(bf16[64,8,256]{2,1,0:T(8,128)(2,1)S(1)} %bitcast.27), channel_id=1, replica_groups=mesh['dp'=16,'expert'=64] {'expert'}, dimensions={0} | all-to-all | bytes 524288 | tf_op jit(solution)/shard_map/all_to_all | solution.py:225
  31.6 0.0 copy-done.1
  31.6 0.0 copy-done.2
  31.6 0.0 copy-done
  31.6 0.5 shard_map.103
  32.1 11.9 %collective-permute-start = (bf16[2,96,1152]{2,1,0:T(8,128)(2,1)S(1)}, bf16[2,96,1152]{2,1,0:T(8,128)(2,1)S(1)}, u32[]{:S(2)}, u32[]{:S(2)}) collective-permute-start(bf16[2,96,1152]{2,1,0:T(8,128)(2,1)S(1)} %get-tuple-element.16), channel_id=1, source_target_pairs={{0,64},{1,961},{2,66},{3,963},{4,68},{5,965},{6,70},{7,967},{8,72}... | collective-permute-start | bytes 1327112 | tf_op jit(solution)/shard_map/ppermute | solution.py:238
  44.1 5.7 %collective-permute-done = bf16[2,96,1152]{2,1,0:T(8,128)(2,1)S(1)} collective-permute-done((bf16[2,96,1152]{2,1,0:T(8,128)(2,1)S(1)}, bf16[2,96,1152]{2,1,0:T(8,128)(2,1)S(1)}, u32[]{:S(2)}, u32[]{:S(2)}) %collective-permute-start) | collective-permute-done | bytes 442400 | tf_op jit(solution)/shard_map/ppermute | solution.py:238
  49.7 0.1 shard_map.104
  49.9 28.8 %all_to_all.16.parts_ref = bf16[8,24,1152]{2,1,0:T(8,128)(2,1)S(1)} all-to-all(bf16[8,24,1152]{2,1,0:T(8,128)(2,1)S(1)} %get-tuple-element.17), channel_id=1, replica_groups={{0,128,256,384,512,640,768,896},{64,192,320,448,576,704,832,960},{1,129..., dimensions={0} | all-to-all | bytes 884736 | tf_op jit(solution)/shard_map/all_to_all | solution.py:247
  78.7 0.1 shard_map.105
  78.8 29.6 %all-gather = bf16[384,1152]{1,0:T(8,128)(2,1)S(1)} all-gather(bf16[24,1152]{1,0:T(8,128)(2,1)S(1)} %shard_map.105), channel_id=2, replica_groups=mesh['dp'=16,'expert'=64] {'dp'}, dimensions={0}, use_global_device_ids=true | all-gather | bytes 940032 | tf_op jit(solution)/shard_map/all_gather | solution.py:249
  108.4 1.1 shard_map.106
  109.5 14.7 %all-to-all-start.2 = ((bf16[64,8,128]{2,1,0:T(8,128)(2,1)}), bf16[64,8,128]{2,1,0:T(8,128)(2,1)S(1)}, u32[]{:S(2)}, u32[]{:S(2)}) async-start(bf16[64,8,128]{2,1,0:T(8,128)(2,1)} %bitcast.10), calls=%async_computation.2 | async-start | bytes 262144 | tf_op jit(solution)/shard_map/all_to_all | solution.py:252
  124.2 1.6 %shard_map.108 = (bf16[256,768]{1,0:T(8,128)(2,1)}, bf16[256,768]{1,0:T(8,128)(2,1)}, bf16[768,256]{1,0:T(8,128)(2,1)}) custom-call(bf16[2,192,1152]{2,1,0:T(8,128)(2,1)S(1)} %bitcast.16, bf16[512,256]{1,0:T(8,128)(2,1)S(1)} %bitcast.18), custom_call_target="tpu_custom_call" | custom-call | flops 226492416 | bytes 2326528 | tf_op jit(solution)/shard_map/pallas_call | solution.py:194
  125.8 8.8 %all-to-all-done.2 = bf16[64,8,128]{2,1,0:T(8,128)(2,1)S(1)} async-done(((bf16[64,8,128]{2,1,0:T(8,128)(2,1)}), bf16[64,8,128]{2,1,0:T(8,128)(2,1)S(1)}, u32[]{:S(2)}, u32[]{:S(2)}) %all-to-all-start.2) | async-done | bytes 131104 | tf_op jit(solution)/shard_map/all_to_all | solution.py:252
  134.5 0.8 shard_map.107
Async XLA Ops:
  0.6 31.0 %copy-start.1 = (bf16[1,256,768]{2,1,0:T(8,128)(2,1)S(1)}, bf16[1,256,768]{2,1,0:T(8,128)(2,1)}, u32[]{:S(2)}) copy-start(bf16[1,256,768]{2,1,0:T(8,128)(2,1)} %param.12) | copy-start | bytes 1179652
  0.6 31.0 %copy-start.2 = (bf16[1,768,256]{2,1,0:T(8,128)(2,1)S(1)}, bf16[1,768,256]{2,1,0:T(8,128)(2,1)}, u32[]{:S(2)}) copy-start(bf16[1,768,256]{2,1,0:T(8,128)(2,1)} %param.13) | copy-start | bytes 1179652
  2.0 29.6 %copy-start = (bf16[1,256,768]{2,1,0:T(8,128)(2,1)S(1)}, bf16[1,256,768]{2,1,0:T(8,128)(2,1)}, u32[]{:S(2)}) copy-start(bf16[1,256,768]{2,1,0:T(8,128)(2,1)} %param.11) | copy-start | bytes 1179652
  32.1 17.6 %collective-permute-start = (bf16[2,96,1152]{2,1,0:T(8,128)(2,1)S(1)}, bf16[2,96,1152]{2,1,0:T(8,128)(2,1)S(1)}, u32[]{:S(2)}, u32[]{:S(2)}) collective-permute-start(bf16[2,96,1152]{2,1,0:T(8,128)(2,1)S(1)} %get-tuple-element.16), channel_id=1, source_target_pairs={{0,64},{1,961},{2,66},{3,963},{4,68},{5,965},{6,70},{7,967},{8,72}... | collective-permute-start | bytes 1327112 | tf_op jit(solution)/shard_map/ppermute | solution.py:238
  109.5 25.1 %all-to-all-start.2 = ((bf16[64,8,128]{2,1,0:T(8,128)(2,1)}), bf16[64,8,128]{2,1,0:T(8,128)(2,1)S(1)}, u32[]{:S(2)}, u32[]{:S(2)}) async-start(bf16[64,8,128]{2,1,0:T(8,128)(2,1)} %bitcast.10), calls=%async_computation.2 | async-start | bytes 262144 | tf_op jit(solution)/shard_map/all_to_all | solution.py:252

commit v4 on v3

--- a/solution.py
+++ b/solution.py
@@ -22,6 +22,10 @@
 DP = 16
 SLOTS = EXPERTS * 8
 SAME_PARITY = [[2 * a + b for a in range(DP // 2)] for b in range(2)]
+CORES = [[2 * chip, 2 * chip + 1] for chip in range(EXPERTS // 2)]
+SAME_CORE = [[2 * chip + core for chip in range(EXPERTS // 2)] for core in range(2)]
+
+
 def partner(dp, expert):
     if expert % 2 == 0:
         return dp ^ 1
@@ -29,7 +33,9 @@
 
 
 PAIRS = [
-    (dp * EXPERTS + expert, partner(dp, expert) * EXPERTS + expert) for dp in range(DP) for expert in range(EXPERTS)
+    [dp * EXPERTS + expert, partner(dp, expert) * EXPERTS + expert]
+    for expert in range(EXPERTS)
+    for dp in range(0, DP, 2)
 ]
 VMEM_LIMIT = 24 * 1024 * 1024
 
@@ -71,10 +77,16 @@
     values = [acts] + [(column(combine_t[k : k + 1, :]) * wide).astype(BF16) for k in range(PICKS)]
     sent = dot(jnp.concatenate(choose, axis=0), jnp.concatenate(values, axis=0), ((0,), (0,)))
     back = [as_bf16(named & (place == 2 * rank + half)) for half in range(2)]
-    return sent.astype(BF16), jnp.concatenate(back, axis=0)
-
-
-def dispatch_kernel(routes, combine, acts, grad_out, sent_ref, back_ref, *scratch):
+    return sent, jnp.concatenate(back, axis=0)
+
+
+def by_core(sent, core):
+    split = sent.reshape(EXPERTS // 2, 2, 8, WIDTH)
+    low, high = split[:, 0], split[:, 1]
+    return jnp.where(core == 0, low, high), jnp.where(core == 0, high, low)
+
+
+def dispatch_kernel(routes, combine, acts, grad_out, own_ref, other_ref, back_ref, *scratch):
     held, arrived = scratch[:4], scratch[4]
     copies = [
         pltpu.make_async_copy(source, place, arrived.at[i])
@@ -84,7 +96,18 @@
         copy.start()
     for copy in copies:
         copy.wait()
-    sent_ref[...], back_ref[...] = dispatch_body(*(place[...] for place in held))
+    sent, back_ref[...] = dispatch_body(*(place[...] for place in held))
+    own, other = by_core(sent, jnp.bitwise_and(lax.axis_index("expert"), 1))
+    own_ref[...] = own.reshape(SLOTS // 2, WIDTH).astype(BF16)
+    other_ref[...] = other.reshape(SLOTS // 2, WIDTH).astype(BF16)
+
+
+def join_kernel(own_ref, taken_ref, out_ref):
+    first = lax.axis_index("expert") % 2 == 0
+    own = own_ref[...].astype(F32)
+    low = jnp.where(first, own, taken_ref[0].astype(F32)).reshape(EXPERTS // 2, 8, WIDTH)
+    high = jnp.where(first, taken_ref[1].astype(F32), own).reshape(EXPERTS // 2, 8, WIDTH)
+    out_ref[...] = jnp.concatenate([low, high], axis=1).reshape(SLOTS, WIDTH).astype(BF16)
 
 
 def take_rows(received_ref, held):
@@ -123,10 +146,12 @@
 
 
 def pair_kernel(own_ref, taken_ref, out_ref, left_ref):
-    total = own_ref[...] + taken_ref[...].astype(F32)
+    dp = lax.axis_index("dp")
+    from_partner = 1 - jnp.bitwise_and(dp, 1)
+    total = own_ref[...] + taken_ref[from_partner].astype(F32)
     out_ref[...] = total.astype(BF16)
-    mine = lax.shift_right_logical(lax.axis_index("dp"), 1)
-    kept = own_ref[mine] + taken_ref[mine].astype(F32)
+    mine = lax.shift_right_logical(dp, 1)
+    kept = own_ref[mine] + taken_ref[from_partner, mine].astype(F32)
     left_ref[...] = kept - kept.astype(BF16).astype(F32)
 
 
@@ -208,9 +233,9 @@
     gate_w, up_w, down_w = w_gate[0], w_up[0], w_down[0]
     matmul = 2 * ROWS * WIDTH * HIDDEN
 
-    sent, back = call(
+    own, other, back = call(
         dispatch_kernel,
-        [((SLOTS, WIDTH), BF16), ((2 * TOK, SLOTS), BF16)],
+        [((SLOTS // 2, WIDTH), BF16), ((SLOTS // 2, WIDTH), BF16), ((2 * TOK, SLOTS), BF16)],
         4 * matmul,
         *(pltpu.with_memory_space_constraint(x, pltpu.HBM) for x in (routes.T, combine.T, acts, grad_out)),
         in_specs=[HBM] * 4,
@@ -222,8 +247,11 @@
             pltpu.SemaphoreType.DMA((4,)),
         ],
     )
-    received = lax.all_to_all(sent.reshape(EXPERTS, 8, WIDTH), "expert", 0, 0, tiled=True)
-    received = received.reshape(SLOTS, WIDTH)
+    taken = lax.all_gather(other, "expert", axis=0, axis_index_groups=CORES)
+    sent = call(join_kernel, [((SLOTS, WIDTH), BF16)], SLOTS * WIDTH, own, taken)
+    received = lax.all_to_all(
+        sent.reshape(EXPERTS // 2, 16, WIDTH), "expert", 0, 0, tiled=True, axis_index_groups=SAME_CORE
+    ).reshape(SLOTS, WIDTH)
 
     own, send = call(
         product_kernel,
@@ -235,14 +263,14 @@
         down_w,
         scratch_shapes=[TAKEN],
     )
-    taken = lax.ppermute(send, ("dp", "expert"), PAIRS)
+    taken = lax.all_gather(send, ("dp", "expert"), axis=0, axis_index_groups=PAIRS)
     eighths = (DP // 2, CHUNK, PACK)
     parts, left = call(
         pair_kernel,
         [(eighths, BF16), ((CHUNK, PACK), F32)],
         ROWS * PACK,
         own.reshape(eighths),
-        taken.reshape(eighths),
+        taken.reshape((2, *eighths)),
     )
     parts = lax.all_to_all(parts, "dp", 0, 0, tiled=True, axis_index_groups=SAME_PARITY)
     block = call(activate_kernel, [((CHUNK, PACK), BF16)], 20 * CHUNK * PACK, parts, left)

time: 136 us -> 134 us (0.985)
  blocking collectives: 88 us -> 101 us
  starting transfers between devices: 26.7 us -> 17.5 us
  waiting for transfers between devices: 14.5 us -> 8.79 us
    all_gather x0 -> x2, blocking collectives: none -> 31.5 us  [the longest x1 15.8 us: on_device(): taken = lax.all_gather(other, 'expert', axis=0, axis_index_groups=CORES)]
    all_to_all x1, blocking collectives: 29.6 us -> 13.3 us  [on_device(): lax.all_to_all(sent.reshape(EXPERTS // 2, 16, WIDTH), 'expert', 0, 0, til...]
    ppermute x1 -> x0, starting transfers between devices: 11.9 us -> none  [on_device(): taken = lax.ppermute(send, ('dp', 'expert'), PAIRS)]
    ppermute x1 -> x0, waiting for transfers between devices: 5.68 us -> none  [on_device(): taken = lax.ppermute(send, ('dp', 'expert'), PAIRS)]
    all_to_all x1, blocking collectives: 28.8 us -> 24.7 us  [on_device(): lax.all_to_all(parts, 'dp', 0, 0, tiled=True, axis_index_groups=SAME_PARITY)]
    all_to_all x1, starting transfers between devices: 14.7 us -> 17.5 us  [on_device(): lax.all_to_all(row_grads.reshape(EXPERTS, 8, 128), 'expert', 0, 0, tiled=...]
    all_gather x1, blocking collectives: 29.6 us -> 31.9 us  [on_device(): packed = lax.all_gather(block, 'dp', axis=0).reshape(2, ROWS, PACK)]
    pallas_call x7 -> x8, Pallas kernels: 5.48 us -> 5.47 us  [call(): pl.pallas_call(kernel, out_shape=shapes if len(shapes) > 1 else shapes[0]...]
  transfers between devices with their start and end apart: 2 -> 1, of which waited for: 2 -> 1; matrix products, arithmetic and copies ran while one was open for 0% -> 0% of each run, Pallas kernels for 1% -> 1%
where the time goes in v4:
time: 134 us
  blocking collectives  101 us (75%)
  starting transfers between devices  17.5 us (13%)
  waiting for transfers between devices  8.79 us (7%)
  Pallas kernels  5.47 us (4%)
    all_gather x1, blocking collectives, on_device(): packed = lax.all_gather(block, 'dp', axis=0).reshape(2, ROWS, PACK)  31.9 us
    all_to_all x1, blocking collectives, on_device(): lax.all_to_all(parts, 'dp', 0, 0, tiled=True, axis_index_groups=SAME_PARITY)  24.7 us
    all_to_all x1, starting transfers between devices, on_device(): lax.all_to_all(row_grads.reshape(EXPERTS, 8, 128), 'expert', 0, 0, tiled=...  17.5 us
    all_gather x1, blocking collectives, on_device(): taken = lax.all_gather(other, 'expert', axis=0, axis_index_groups=CORES)  15.8 us
    all_gather x1, blocking collectives, on_device(): lax.all_gather(send, ('dp', 'expert'), axis=0, axis_index_groups=PAIRS)  15.7 us
    all_to_all x1, blocking collectives, on_device(): lax.all_to_all(sent.reshape(EXPERTS // 2, 16, WIDTH), 'expert', 0, 0, til...  13.3 us
    all_to_all x1, waiting for transfers between devices, on_device(): lax.all_to_all(row_grads.reshape(EXPERTS, 8, 128), 'expert', 0, 0, tiled=...  8.79 us
    pallas_call x8, Pallas kernels, call(): pl.pallas_call(kernel, out_shape=shapes if len(shapes) > 1 else shapes[0]...  5.47 us
  transfers between devices with their start and end apart: 1, of which 1 were waited for; matrix products, arithmetic and copies ran while one was open for 0% of the time, Pallas kernels for 1%

profile of v4, /device:TPU:1, one launch (start us, length us, event | category | flops | bytes accessed | tf_op | source)
XLA Modules:
  0.0 133.9 jit_solution(5358103064102923303)
XLA Ops:
  0.6 1.3 shard_map.102
  2.0 15.8 %all-gather = bf16[512,256]{1,0:T(8,128)(2,1)S(1)} all-gather(bf16[256,256]{1,0:T(8,128)(2,1)S(1)} %get-tuple-element.16), channel_id=2, replica_groups={{0,1},{2,3},{4,5},{6,7},{8,9},{10,11},{12,13},{14,15},{16,17},{18,19},{..., dimensions={0}, use_global_device_ids=true | all-gather | bytes 393216 | tf_op jit(solution)/shard_map/all_gather | solution.py:250
  17.7 0.0 copy-start.1
  17.7 0.0 copy-start.2
  17.7 0.1 shard_map.103
  17.8 0.0 copy-start
  17.8 13.3 %all_to_all.15 = bf16[32,16,256]{2,1,0:T(8,128)(2,1)S(1)} all-to-all(bf16[32,16,256]{2,1,0:T(8,128)(2,1)S(1)} %bitcast.26), channel_id=1, replica_groups={{0,2,4,6,8,10,12,14,16,18,20,22,24,26,28,30,32,34,36,38,40,42,44,46,48,..., dimensions={0} | all-to-all | bytes 524288 | tf_op jit(solution)/shard_map/all_to_all | solution.py:252
  31.2 0.0 copy-done.1
  31.2 0.0 copy-done.2
  31.2 0.0 copy-done
  31.2 0.5 shard_map.104
  31.7 15.7 %all-gather.1 = bf16[4,96,1152]{2,1,0:T(8,128)(2,1)S(1)} all-gather(bf16[2,96,1152]{2,1,0:T(8,128)(2,1)S(1)} %get-tuple-element.18), channel_id=3, replica_groups={{0,64},{128,192},{256,320},{384,448},{512,576},{640,704},{768,832},{896..., dimensions={0}, use_global_device_ids=true | all-gather | bytes 1327104 | tf_op jit(solution)/shard_map/all_gather | solution.py:266
  47.4 0.1 shard_map.105
  47.5 24.7 %all_to_all.16.parts_ref = bf16[8,24,1152]{2,1,0:T(8,128)(2,1)S(1)} all-to-all(bf16[8,24,1152]{2,1,0:T(8,128)(2,1)S(1)} %get-tuple-element.19), channel_id=1, replica_groups={{0,128,256,384,512,640,768,896},{64,192,320,448,576,704,832,960},{1,129..., dimensions={0} | all-to-all | bytes 884736 | tf_op jit(solution)/shard_map/all_to_all | solution.py:275
  72.2 0.1 shard_map.106
  72.3 31.9 %all-gather.2 = bf16[384,1152]{1,0:T(8,128)(2,1)S(1)} all-gather(bf16[24,1152]{1,0:T(8,128)(2,1)S(1)} %shard_map.106), channel_id=4, replica_groups=mesh['dp'=16,'expert'=64] {'dp'}, dimensions={0}, use_global_device_ids=true | all-gather | bytes 940032 | tf_op jit(solution)/shard_map/all_gather | solution.py:277
  104.2 1.1 shard_map.107
  105.3 17.5 %all-to-all-start.2 = ((bf16[64,8,128]{2,1,0:T(8,128)(2,1)}), bf16[64,8,128]{2,1,0:T(8,128)(2,1)S(1)}, u32[]{:S(2)}, u32[]{:S(2)}) async-start(bf16[64,8,128]{2,1,0:T(8,128)(2,1)} %bitcast.11), calls=%async_computation.2 | async-start | bytes 262144 | tf_op jit(solution)/shard_map/all_to_all | solution.py:280
  122.8 1.6 %shard_map.109 = (bf16[256,768]{1,0:T(8,128)(2,1)}, bf16[256,768]{1,0:T(8,128)(2,1)}, bf16[768,256]{1,0:T(8,128)(2,1)}) custom-call(bf16[2,192,1152]{2,1,0:T(8,128)(2,1)S(1)} %bitcast.17, bf16[512,256]{1,0:T(8,128)(2,1)S(1)} %bitcast.20), custom_call_target="tpu_custom_call" | custom-call | flops 226492416 | bytes 2326528 | tf_op jit(solution)/shard_map/pallas_call | solution.py:219
  124.4 8.8 %all-to-all-done.2 = bf16[64,8,128]{2,1,0:T(8,128)(2,1)S(1)} async-done(((bf16[64,8,128]{2,1,0:T(8,128)(2,1)}), bf16[64,8,128]{2,1,0:T(8,128)(2,1)S(1)}, u32[]{:S(2)}, u32[]{:S(2)}) %all-to-all-start.2) | async-done | bytes 131104 | tf_op jit(solution)/shard_map/all_to_all | solution.py:280
  133.2 0.8 shard_map.108
Async XLA Ops:
  17.7 13.4 %copy-start.1 = (bf16[1,256,768]{2,1,0:T(8,128)(2,1)S(1)}, bf16[1,256,768]{2,1,0:T(8,128)(2,1)}, u32[]{:S(2)}) copy-start(bf16[1,256,768]{2,1,0:T(8,128)(2,1)} %param.12) | copy-start | bytes 1179652
  17.7 13.4 %copy-start.2 = (bf16[1,768,256]{2,1,0:T(8,128)(2,1)S(1)}, bf16[1,768,256]{2,1,0:T(8,128)(2,1)}, u32[]{:S(2)}) copy-start(bf16[1,768,256]{2,1,0:T(8,128)(2,1)} %param.13) | copy-start | bytes 1179652
  17.8 13.4 %copy-start = (bf16[1,256,768]{2,1,0:T(8,128)(2,1)S(1)}, bf16[1,256,768]{2,1,0:T(8,128)(2,1)}, u32[]{:S(2)}) copy-start(bf16[1,256,768]{2,1,0:T(8,128)(2,1)} %param.11) | copy-start | bytes 1179652
  105.3 27.9 %all-to-all-start.2 = ((bf16[64,8,128]{2,1,0:T(8,128)(2,1)}), bf16[64,8,128]{2,1,0:T(8,128)(2,1)S(1)}, u32[]{:S(2)}, u32[]{:S(2)}) async-start(bf16[64,8,128]{2,1,0:T(8,128)(2,1)} %bitcast.11), calls=%async_computation.2 | async-start | bytes 262144 | tf_op jit(solution)/shard_map/all_to_all | solution.py:280

commit v5 on v3

--- a/solution.py
+++ b/solution.py
@@ -22,6 +22,7 @@
 DP = 16
 SLOTS = EXPERTS * 8
 SAME_PARITY = [[2 * a + b for a in range(DP // 2)] for b in range(2)]
+
 def partner(dp, expert):
     if expert % 2 == 0:
         return dp ^ 1
@@ -29,7 +30,9 @@
 
 
 PAIRS = [
-    (dp * EXPERTS + expert, partner(dp, expert) * EXPERTS + expert) for dp in range(DP) for expert in range(EXPERTS)
+    [dp * EXPERTS + expert, partner(dp, expert) * EXPERTS + expert]
+    for expert in range(EXPERTS)
+    for dp in range(0, DP, 2)
 ]
 VMEM_LIMIT = 24 * 1024 * 1024
 
@@ -123,10 +126,12 @@
 
 
 def pair_kernel(own_ref, taken_ref, out_ref, left_ref):
-    total = own_ref[...] + taken_ref[...].astype(F32)
+    dp = lax.axis_index("dp")
+    from_partner = 1 - jnp.bitwise_and(dp, 1)
+    total = own_ref[...] + taken_ref[from_partner].astype(F32)
     out_ref[...] = total.astype(BF16)
-    mine = lax.shift_right_logical(lax.axis_index("dp"), 1)
-    kept = own_ref[mine] + taken_ref[mine].astype(F32)
+    mine = lax.shift_right_logical(dp, 1)
+    kept = own_ref[mine] + taken_ref[from_partner, mine].astype(F32)
     left_ref[...] = kept - kept.astype(BF16).astype(F32)
 
 
@@ -235,14 +240,14 @@
         down_w,
         scratch_shapes=[TAKEN],
     )
-    taken = lax.ppermute(send, ("dp", "expert"), PAIRS)
+    taken = lax.all_gather(send, ("dp", "expert"), axis=0, axis_index_groups=PAIRS)
     eighths = (DP // 2, CHUNK, PACK)
     parts, left = call(
         pair_kernel,
         [(eighths, BF16), ((CHUNK, PACK), F32)],
         ROWS * PACK,
         own.reshape(eighths),
-        taken.reshape(eighths),
+        taken.reshape((2, *eighths)),
     )
     parts = lax.all_to_all(parts, "dp", 0, 0, tiled=True, axis_index_groups=SAME_PARITY)
     block = call(activate_kernel, [((CHUNK, PACK), BF16)], 20 * CHUNK * PACK, parts, left)

time: 136 us -> 134 us (0.985)
  blocking collectives: 88 us -> 104 us
  starting transfers between devices: 26.7 us -> 14.7 us
  waiting for transfers between devices: 14.5 us -> 8.79 us
    all_gather x0 -> x1, blocking collectives: none -> 16.4 us  [on_device(): lax.all_gather(send, ('dp', 'expert'), axis=0, axis_index_groups=PAIRS)]
    ppermute x1 -> x0, starting transfers between devices: 11.9 us -> none  [on_device(): taken = lax.ppermute(send, ('dp', 'expert'), PAIRS)]
    ppermute x1 -> x0, waiting for transfers between devices: 5.68 us -> none  [on_device(): taken = lax.ppermute(send, ('dp', 'expert'), PAIRS)]
  transfers between devices with their start and end apart: 2 -> 1, of which waited for: 2 -> 1; matrix products, arithmetic and copies ran while one was open for 0% -> 0% of each run, Pallas kernels for 1% -> 1%
where the time goes in v5:
time: 134 us
  blocking collectives  104 us (78%)
  starting transfers between devices  14.7 us (11%)
  waiting for transfers between devices  8.79 us (7%)
  Pallas kernels  5.47 us (4%)
    all_gather x1, blocking collectives, on_device(): packed = lax.all_gather(block, 'dp', axis=0).reshape(2, ROWS, PACK)  29.6 us
    all_to_all x1, blocking collectives, on_device(): lax.all_to_all(sent.reshape(EXPERTS, 8, WIDTH), 'expert', 0, 0, tiled=True)  29.6 us
    all_to_all x1, blocking collectives, on_device(): lax.all_to_all(parts, 'dp', 0, 0, tiled=True, axis_index_groups=SAME_PARITY)  28.8 us
    all_gather x1, blocking collectives, on_device(): lax.all_gather(send, ('dp', 'expert'), axis=0, axis_index_groups=PAIRS)  16.4 us
    all_to_all x1, starting transfers between devices, on_device(): lax.all_to_all(row_grads.reshape(EXPERTS, 8, 128), 'expert', 0, 0, tiled=...  14.7 us
    all_to_all x1, waiting for transfers between devices, on_device(): lax.all_to_all(row_grads.reshape(EXPERTS, 8, 128), 'expert', 0, 0, tiled=...  8.79 us
    pallas_call x7, Pallas kernels, call(): pl.pallas_call(kernel, out_shape=shapes if len(shapes) > 1 else shapes[0]...  5.47 us
  transfers between devices with their start and end apart: 1, of which 1 were waited for; matrix products, arithmetic and copies ran while one was open for 0% of the time, Pallas kernels for 1%

profile of v5, /device:TPU:1, one launch (start us, length us, event | category | flops | bytes accessed | tf_op | source)
XLA Modules:
  0.0 134.1 jit_solution(15097821285521649988)
XLA Ops:
  0.6 0.0 copy-start.1
  0.6 0.0 copy-start.2
  0.7 1.4 %shard_map.102 = (bf16[512,256]{1,0:T(8,128)(2,1)S(1)}, bf16[32,512]{1,0:T(8,128)(2,1)S(1)}) custom-call(s32[8,16]{1,0:T(8,128)} %bitcast.31, f32[8,16]{1,0:T(8,128)} %bitcast.32, bf16[16,256]{1,0:T(8,128)(2,1)} %acts.1, bf16[16,256]{1,0:T(8,128)(2,1)} %grad_out.1), custom_call_target="tpu_custom_call" | custom-call | flops 301989888 | bytes 312320 | tf_op jit(solution)/shard_map/pallas_call | solution.py:199
  2.0 0.0 copy-start
  2.1 29.6 %all_to_all.15 = bf16[64,8,256]{2,1,0:T(8,128)(2,1)S(1)} all-to-all(bf16[64,8,256]{2,1,0:T(8,128)(2,1)S(1)} %bitcast.27), channel_id=1, replica_groups=mesh['dp'=16,'expert'=64] {'expert'}, dimensions={0} | all-to-all | bytes 524288 | tf_op jit(solution)/shard_map/all_to_all | solution.py:230
  31.6 0.0 copy-done.1
  31.6 0.0 copy-done.2
  31.6 0.0 copy-done
  31.6 0.5 shard_map.103
  32.1 16.4 %all-gather = bf16[4,96,1152]{2,1,0:T(8,128)(2,1)S(1)} all-gather(bf16[2,96,1152]{2,1,0:T(8,128)(2,1)S(1)} %get-tuple-element.16), channel_id=2, replica_groups={{0,64},{128,192},{256,320},{384,448},{512,576},{640,704},{768,832},{896..., dimensions={0}, use_global_device_ids=true | all-gather | bytes 1327104 | tf_op jit(solution)/shard_map/all_gather | solution.py:243
  48.5 0.1 shard_map.104
  48.6 28.8 %all_to_all.16.parts_ref = bf16[8,24,1152]{2,1,0:T(8,128)(2,1)S(1)} all-to-all(bf16[8,24,1152]{2,1,0:T(8,128)(2,1)S(1)} %get-tuple-element.17), channel_id=1, replica_groups={{0,128,256,384,512,640,768,896},{64,192,320,448,576,704,832,960},{1,129..., dimensions={0} | all-to-all | bytes 884736 | tf_op jit(solution)/shard_map/all_to_all | solution.py:252
  77.4 0.1 shard_map.105
  77.5 29.6 %all-gather.1 = bf16[384,1152]{1,0:T(8,128)(2,1)S(1)} all-gather(bf16[24,1152]{1,0:T(8,128)(2,1)S(1)} %shard_map.105), channel_id=3, replica_groups=mesh['dp'=16,'expert'=64] {'dp'}, dimensions={0}, use_global_device_ids=true | all-gather | bytes 940032 | tf_op jit(solution)/shard_map/all_gather | solution.py:254
  107.1 1.1 shard_map.106
  108.2 14.7 %all-to-all-start.2 = ((bf16[64,8,128]{2,1,0:T(8,128)(2,1)}), bf16[64,8,128]{2,1,0:T(8,128)(2,1)S(1)}, u32[]{:S(2)}, u32[]{:S(2)}) async-start(bf16[64,8,128]{2,1,0:T(8,128)(2,1)} %bitcast.10), calls=%async_computation.2 | async-start | bytes 262144 | tf_op jit(solution)/shard_map/all_to_all | solution.py:257
  123.0 1.6 %shard_map.108 = (bf16[256,768]{1,0:T(8,128)(2,1)}, bf16[256,768]{1,0:T(8,128)(2,1)}, bf16[768,256]{1,0:T(8,128)(2,1)}) custom-call(bf16[2,192,1152]{2,1,0:T(8,128)(2,1)S(1)} %bitcast.16, bf16[512,256]{1,0:T(8,128)(2,1)S(1)} %bitcast.19), custom_call_target="tpu_custom_call" | custom-call | flops 226492416 | bytes 2326528 | tf_op jit(solution)/shard_map/pallas_call | solution.py:199
  124.5 8.8 %all-to-all-done.2 = bf16[64,8,128]{2,1,0:T(8,128)(2,1)S(1)} async-done(((bf16[64,8,128]{2,1,0:T(8,128)(2,1)}), bf16[64,8,128]{2,1,0:T(8,128)(2,1)S(1)}, u32[]{:S(2)}, u32[]{:S(2)}) %all-to-all-start.2) | async-done | bytes 131104 | tf_op jit(solution)/shard_map/all_to_all | solution.py:257
  133.3 0.8 shard_map.107
Async XLA Ops:
  0.6 31.0 %copy-start.1 = (bf16[1,256,768]{2,1,0:T(8,128)(2,1)S(1)}, bf16[1,256,768]{2,1,0:T(8,128)(2,1)}, u32[]{:S(2)}) copy-start(bf16[1,256,768]{2,1,0:T(8,128)(2,1)} %param.12) | copy-start | bytes 1179652
  0.6 31.0 %copy-start.2 = (bf16[1,768,256]{2,1,0:T(8,128)(2,1)S(1)}, bf16[1,768,256]{2,1,0:T(8,128)(2,1)}, u32[]{:S(2)}) copy-start(bf16[1,768,256]{2,1,0:T(8,128)(2,1)} %param.13) | copy-start | bytes 1179652
  2.0 29.6 %copy-start = (bf16[1,256,768]{2,1,0:T(8,128)(2,1)S(1)}, bf16[1,256,768]{2,1,0:T(8,128)(2,1)}, u32[]{:S(2)}) copy-start(bf16[1,256,768]{2,1,0:T(8,128)(2,1)} %param.11) | copy-start | bytes 1179652
  108.2 25.1 %all-to-all-start.2 = ((bf16[64,8,128]{2,1,0:T(8,128)(2,1)}), bf16[64,8,128]{2,1,0:T(8,128)(2,1)S(1)}, u32[]{:S(2)}, u32[]{:S(2)}) async-start(bf16[64,8,128]{2,1,0:T(8,128)(2,1)} %bitcast.10), calls=%async_computation.2 | async-start | bytes 262144 | tf_op jit(solution)/shard_map/all_to_all | solution.py:257

commit v6 on v5

--- a/solution.py
+++ b/solution.py
@@ -189,8 +189,9 @@
     return jnp.concatenate([left, right], axis=1).astype(BF16)
 
 
-def combine_kernel(back_ref, returned_ref, out_ref):
-    out_ref[...] = combine_body(back_ref[...], returned_ref[...])
+def final_kernel(packed_ref, received_ref, back_ref, returned_ref, acts_ref, gate_ref, up_ref, down_ref, held):
+    acts_ref[...] = combine_body(back_ref[...], returned_ref[...])
+    weight_kernel(packed_ref, received_ref, gate_ref, up_ref, down_ref, held)
 
 
 def call(kernel, outs, flops, *operands, **options):
@@ -255,16 +256,15 @@
 
     row_grads = call(row_grad_kernel, [((SLOTS, 128), BF16)], 2 * matmul, packed, gate_w, up_w, scratch_shapes=[pltpu.VMEM((SLOTS, 128), F32)])
     returned = lax.all_to_all(row_grads.reshape(EXPERTS, 8, 128), "expert", 0, 0, tiled=True)
-    new_gate, new_up, new_down = call(
-        weight_kernel,
-        [((WIDTH, HIDDEN), BF16), ((WIDTH, HIDDEN), BF16), ((HIDDEN, WIDTH), BF16)],
+    grad_acts, new_gate, new_up, new_down = call(
+        final_kernel,
+        [((TOK, WIDTH), BF16), ((WIDTH, HIDDEN), BF16), ((WIDTH, HIDDEN), BF16), ((HIDDEN, WIDTH), BF16)],
         3 * matmul,
         packed,
         received,
+        back,
+        returned.reshape(SLOTS, 128),
         scratch_shapes=[TAKEN],
-    )
-    grad_acts = call(
-        combine_kernel, [((TOK, WIDTH), BF16)], 4 * TOK * SLOTS * 128, back, returned.reshape(SLOTS, 128)
     )
     return grad_acts, new_gate[None], new_up[None], new_down[None]
 

time: 134 us -> 134 us (level)
  blocking collectives: 104 us -> 129 us
  starting transfers between devices: 14.7 us -> 0 us
  waiting for transfers between devices: 8.79 us -> 0 us
  Pallas kernels: 5.47 us -> 4.05 us
    all_to_all x0 -> x1, blocking collectives: none -> 24.9 us  [on_device(): lax.all_to_all(row_grads.reshape(EXPERTS, 8, 128), 'expert', 0, 0, tiled=...]
    all_to_all x1 -> x0, starting transfers between devices: 14.7 us -> none  [on_device(): lax.all_to_all(row_grads.reshape(EXPERTS, 8, 128), 'expert', 0, 0, tiled=...]
    all_to_all x1 -> x0, waiting for transfers between devices: 8.79 us -> none  [on_device(): lax.all_to_all(row_grads.reshape(EXPERTS, 8, 128), 'expert', 0, 0, tiled=...]
    pallas_call x7 -> x6, Pallas kernels: 5.47 us -> 4.05 us  [call(): pl.pallas_call(kernel, out_shape=shapes if len(shapes) > 1 else shapes[0]...]
  transfers between devices with their start and end apart: 1 -> 0, of which waited for: 1 -> 0; matrix products, arithmetic and copies ran while one was open for 0% -> 0% of each run, Pallas kernels for 1% -> 0%
where the time goes in v6:
time: 134 us
  blocking collectives  129 us (96%)
  Pallas kernels  4.05 us (3%)
    all_gather x1, blocking collectives, on_device(): packed = lax.all_gather(block, 'dp', axis=0).reshape(2, ROWS, PACK)  29.6 us
    all_to_all x1, blocking collectives, on_device(): lax.all_to_all(sent.reshape(EXPERTS, 8, WIDTH), 'expert', 0, 0, tiled=True)  29.6 us
    all_to_all x1, blocking collectives, on_device(): lax.all_to_all(parts, 'dp', 0, 0, tiled=True, axis_index_groups=SAME_PARITY)  28.8 us
    all_to_all x1, blocking collectives, on_device(): lax.all_to_all(row_grads.reshape(EXPERTS, 8, 128), 'expert', 0, 0, tiled=...  24.9 us
    all_gather x1, blocking collectives, on_device(): lax.all_gather(send, ('dp', 'expert'), axis=0, axis_index_groups=PAIRS)  16.4 us
    pallas_call x6, Pallas kernels, call(): pl.pallas_call(kernel, out_shape=shapes if len(shapes) > 1 else shapes[0]...  4.05 us

profile of v6, /device:TPU:1, one launch (start us, length us, event | category | flops | bytes accessed | tf_op | source)
XLA Modules:
  0.0 134.0 jit_solution(12205700859480538705)
XLA Ops:
  0.6 0.0 copy-start.1
  0.6 0.0 copy-start.2
  0.7 1.4 %shard_map.102 = (bf16[512,256]{1,0:T(8,128)(2,1)S(1)}, bf16[32,512]{1,0:T(8,128)(2,1)S(1)}) custom-call(s32[8,16]{1,0:T(8,128)} %bitcast.32, f32[8,16]{1,0:T(8,128)} %bitcast.33, bf16[16,256]{1,0:T(8,128)(2,1)} %acts.1, bf16[16,256]{1,0:T(8,128)(2,1)} %grad_out.1), custom_call_target="tpu_custom_call" | custom-call | flops 301989888 | bytes 312320 | tf_op jit(solution)/shard_map/pallas_call | solution.py:200
  2.0 0.0 copy-start
  2.1 29.6 %all_to_all.15 = bf16[64,8,256]{2,1,0:T(8,128)(2,1)S(1)} all-to-all(bf16[64,8,256]{2,1,0:T(8,128)(2,1)S(1)} %bitcast.28), channel_id=1, replica_groups=mesh['dp'=16,'expert'=64] {'expert'}, dimensions={0} | all-to-all | bytes 524288 | tf_op jit(solution)/shard_map/all_to_all | solution.py:231
  31.6 0.0 copy-done.1
  31.6 0.0 copy-done.2
  31.6 0.0 copy-done
  31.6 0.5 shard_map.103
  32.1 16.4 %all-gather = bf16[4,96,1152]{2,1,0:T(8,128)(2,1)S(1)} all-gather(bf16[2,96,1152]{2,1,0:T(8,128)(2,1)S(1)} %get-tuple-element.16), channel_id=2, replica_groups={{0,64},{128,192},{256,320},{384,448},{512,576},{640,704},{768,832},{896..., dimensions={0}, use_global_device_ids=true | all-gather | bytes 1327104 | tf_op jit(solution)/shard_map/all_gather | solution.py:244
  48.5 0.1 shard_map.104
  48.6 28.8 %all_to_all.16.parts_ref = bf16[8,24,1152]{2,1,0:T(8,128)(2,1)S(1)} all-to-all(bf16[8,24,1152]{2,1,0:T(8,128)(2,1)S(1)} %get-tuple-element.17), channel_id=1, replica_groups={{0,128,256,384,512,640,768,896},{64,192,320,448,576,704,832,960},{1,129..., dimensions={0} | all-to-all | bytes 884736 | tf_op jit(solution)/shard_map/all_to_all | solution.py:253
  77.4 0.1 shard_map.105
  77.5 29.6 %all-gather.1 = bf16[384,1152]{1,0:T(8,128)(2,1)S(1)} all-gather(bf16[24,1152]{1,0:T(8,128)(2,1)S(1)} %shard_map.105), channel_id=3, replica_groups=mesh['dp'=16,'expert'=64] {'dp'}, dimensions={0}, use_global_device_ids=true | all-gather | bytes 940032 | tf_op jit(solution)/shard_map/all_gather | solution.py:255
  107.1 0.4 shard_map.106
  107.6 24.9 %all_to_all.17 = bf16[64,8,128]{2,1,0:T(8,128)(2,1)S(1)} all-to-all(bf16[64,8,128]{2,1,0:T(8,128)(2,1)S(1)} %bitcast.26), channel_id=1, replica_groups=mesh['dp'=16,'expert'=64] {'expert'}, dimensions={0} | all-to-all | bytes 262144 | tf_op jit(solution)/shard_map/all_to_all | solution.py:258
  132.5 1.6 %shard_map.107 = (bf16[16,256]{1,0:T(8,128)(2,1)}, bf16[256,768]{1,0:T(8,128)(2,1)}, bf16[256,768]{1,0:T(8,128)(2,1)}, bf16[768,256]{1,0:T(8,128)(2,1)}) custom-call(bf16[2,192,1152]{2,1,0:T(8,128)(2,1)S(1)} %bitcast.16, bf16[512,256]{1,0:T(8,128)(2,1)S(1)} %bitcast.19, bf16[32,512]{1,0:T(8,128)(2,1)S(1)} %get-tuple-element.19.back_ref, ...), custom_call_target="tpu_custom_call" | custom-call | flops 226492416 | bytes 2498560 | tf_op jit(solution)/shard_map/pallas_call | solution.py:200
Async XLA Ops:
  0.6 31.0 %copy-start.1 = (bf16[1,256,768]{2,1,0:T(8,128)(2,1)S(1)}, bf16[1,256,768]{2,1,0:T(8,128)(2,1)}, u32[]{:S(2)}) copy-start(bf16[1,256,768]{2,1,0:T(8,128)(2,1)} %param.12) | copy-start | bytes 1179652
  0.6 31.0 %copy-start.2 = (bf16[1,768,256]{2,1,0:T(8,128)(2,1)S(1)}, bf16[1,768,256]{2,1,0:T(8,128)(2,1)}, u32[]{:S(2)}) copy-start(bf16[1,768,256]{2,1,0:T(8,128)(2,1)} %param.13) | copy-start | bytes 1179652
  2.0 29.6 %copy-start = (bf16[1,256,768]{2,1,0:T(8,128)(2,1)S(1)}, bf16[1,256,768]{2,1,0:T(8,128)(2,1)}, u32[]{:S(2)}) copy-start(bf16[1,256,768]{2,1,0:T(8,128)(2,1)} %param.11) | copy-start | bytes 1179652

commit v7 on v6

--- a/solution.py
+++ b/solution.py
@@ -21,19 +21,20 @@
 CHUNK = 24
 DP = 16
 SLOTS = EXPERTS * 8
-SAME_PARITY = [[2 * a + b for a in range(DP // 2)] for b in range(2)]
-
-def partner(dp, expert):
-    if expert % 2 == 0:
-        return dp ^ 1
-    return (dp + 1) % DP if dp % 2 else (dp - 1) % DP
-
-
-PAIRS = [
-    [dp * EXPERTS + expert, partner(dp, expert) * EXPERTS + expert]
-    for expert in range(EXPERTS)
-    for dp in range(0, DP, 2)
-]
+QUARTER = DP // 4
+FAR = [[4 * a + low for a in range(QUARTER)] for low in range(4)]
+
+
+def pairs(distance):
+    firsts = [dp for dp in range(DP) if not dp & distance]
+    sign = [distance, -distance]
+    return [
+        [dp * EXPERTS + expert, (dp + sign[expert % 2]) % DP * EXPERTS + expert]
+        for expert in range(EXPERTS)
+        for dp in firsts
+    ]
+
+
 VMEM_LIMIT = 24 * 1024 * 1024
 
 
@@ -125,21 +126,25 @@
         send_ref[half] = other.astype(BF16)
 
 
-def pair_kernel(own_ref, taken_ref, out_ref, left_ref):
+def first_kernel(own_ref, taken_ref, keep_ref, send_ref):
     dp = lax.axis_index("dp")
     from_partner = 1 - jnp.bitwise_and(dp, 1)
-    total = own_ref[...] + taken_ref[from_partner].astype(F32)
-    out_ref[...] = total.astype(BF16)
-    mine = lax.shift_right_logical(dp, 1)
-    kept = own_ref[mine] + taken_ref[from_partner, mine].astype(F32)
-    left_ref[...] = kept - kept.astype(BF16).astype(F32)
-
-
-def activate_body(parts, left):
-    total = [parts[i].astype(F32) for i in range(8)]
+    mine = jnp.bitwise_and(lax.shift_right_logical(dp, 1), 1)
+    for i in range(QUARTER):
+        keep_ref[i] = own_ref[i, mine] + taken_ref[from_partner, i, mine].astype(F32)
+        send_ref[i] = (own_ref[i, 1 - mine] + taken_ref[from_partner, i, 1 - mine].astype(F32)).astype(BF16)
+
+
+def second_kernel(own_ref, taken_ref, out_ref):
+    from_partner = 1 - jnp.bitwise_and(lax.shift_right_logical(lax.axis_index("dp"), 1), 1)
+    out_ref[...] = own_ref[...] + taken_ref[from_partner].astype(F32)
+
+
+def activate_body(parts):
+    total = [parts[i] for i in range(QUARTER)]
     while len(total) > 1:
         total = [total[i] + total[i + 1] for i in range(0, len(total), 2)]
-    total = total[0] + left
+    total = total[0]
     pre_gate, pre_up, hidden_grad = total[:, :HALF], total[:, HALF : 2 * HALF], total[:, 2 * HALF :]
     sigmoid_gate = jax.nn.sigmoid(pre_gate)
     silu_gate = pre_gate * sigmoid_gate
@@ -149,8 +154,8 @@
     return jnp.concatenate([gate_grad, up_grad, hidden], axis=1).astype(BF16)
 
 
-def activate_kernel(parts_ref, left_ref, out_ref):
-    out_ref[...] = activate_body(parts_ref[...], left_ref[...])
+def activate_kernel(parts_ref, out_ref):
+    out_ref[...] = activate_body(parts_ref[...])
 
 
 def row_grad_body(packed, w_gate, w_up):
@@ -241,17 +246,20 @@
         down_w,
         scratch_shapes=[TAKEN],
     )
-    taken = lax.all_gather(send, ("dp", "expert"), axis=0, axis_index_groups=PAIRS)
-    eighths = (DP // 2, CHUNK, PACK)
-    parts, left = call(
-        pair_kernel,
-        [(eighths, BF16), ((CHUNK, PACK), F32)],
+    mesh_axes = ("dp", "expert")
+    taken = lax.all_gather(send, mesh_axes, axis=0, axis_index_groups=pairs(1))
+    eighths, quarters = (QUARTER, 2, CHUNK, PACK), (QUARTER, CHUNK, PACK)
+    keep, send = call(
+        first_kernel,
+        [(quarters, F32), (quarters, BF16)],
         ROWS * PACK,
         own.reshape(eighths),
         taken.reshape((2, *eighths)),
     )
-    parts = lax.all_to_all(parts, "dp", 0, 0, tiled=True, axis_index_groups=SAME_PARITY)
-    block = call(activate_kernel, [((CHUNK, PACK), BF16)], 20 * CHUNK * PACK, parts, left)
+    taken = lax.all_gather(send, mesh_axes, axis=0, axis_index_groups=pairs(2))
+    parts = call(second_kernel, [(quarters, F32)], ROWS * PACK // 2, keep, taken)
+    parts = lax.all_to_all(parts, "dp", 0, 0, tiled=True, axis_index_groups=FAR)
+    block = call(activate_kernel, [((CHUNK, PACK), BF16)], 20 * CHUNK * PACK, parts)
     packed = lax.all_gather(block, "dp", axis=0).reshape(2, ROWS, PACK)
 
     row_grads = call(row_grad_kernel, [((SLOTS, 128), BF16)], 2 * matmul, packed, gate_w, up_w, scratch_shapes=[pltpu.VMEM((SLOTS, 128), F32)])

time: 134 us -> 144 us (1.075)
  blocking collectives: 129 us -> 138 us
    all_gather x1 -> x2, blocking collectives: 16.4 us -> 24.7 us  [the longest x1 16.5 us: on_device(): taken = lax.all_gather(send, mesh_axes, axis=0, axis_index_groups=pairs(1))]
    all_gather x1, blocking collectives: 29.6 us -> 33.8 us  [on_device(): packed = lax.all_gather(block, 'dp', axis=0).reshape(2, ROWS, PACK)]
    all_to_all x1, blocking collectives: 28.8 us -> 25.6 us  [on_device(): parts = lax.all_to_all(parts, 'dp', 0, 0, tiled=True, axis_index_groups=FAR)]
    pallas_call x6 -> x7, Pallas kernels: 4.05 us -> 4.03 us  [call(): pl.pallas_call(kernel, out_shape=shapes if len(shapes) > 1 else shapes[0]...]
where the time goes in v7:
time: 144 us; the launch traced here: 143 us
  blocking collectives  138 us (96%)
  Pallas kernels  4.03 us (3%)
    all_gather x1, blocking collectives, on_device(): packed = lax.all_gather(block, 'dp', axis=0).reshape(2, ROWS, PACK)  33.8 us
    all_to_all x1, blocking collectives, on_device(): lax.all_to_all(sent.reshape(EXPERTS, 8, WIDTH), 'expert', 0, 0, tiled=True)  29.6 us
    all_to_all x1, blocking collectives, on_device(): parts = lax.all_to_all(parts, 'dp', 0, 0, tiled=True, axis_index_groups=FAR)  25.6 us
    all_to_all x1, blocking collectives, on_device(): lax.all_to_all(row_grads.reshape(EXPERTS, 8, 128), 'expert', 0, 0, tiled=...  24.8 us
    all_gather x1, blocking collectives, on_device(): taken = lax.all_gather(send, mesh_axes, axis=0, axis_index_groups=pairs(1))  16.5 us
    all_gather x1, blocking collectives, on_device(): taken = lax.all_gather(send, mesh_axes, axis=0, axis_index_groups=pairs(2))  8.16 us
    pallas_call x7, Pallas kernels, call(): pl.pallas_call(kernel, out_shape=shapes if len(shapes) > 1 else shapes[0]...  4.03 us

profile of v7, /device:TPU:1, one launch (start us, length us, event | category | flops | bytes accessed | tf_op | source)
XLA Modules:
  0.0 143.2 jit_solution(11845213952923529380)
XLA Ops:
  0.6 0.0 copy-start.1
  0.6 0.0 copy-start.2
  0.7 1.4 shard_map.102
  2.0 0.0 copy-start
  2.1 29.6 %all_to_all.15 = bf16[64,8,256]{2,1,0:T(8,128)(2,1)S(1)} all-to-all(bf16[64,8,256]{2,1,0:T(8,128)(2,1)S(1)} %bitcast.30), channel_id=1, replica_groups=mesh['dp'=16,'expert'=64] {'expert'}, dimensions={0} | all-to-all | bytes 524288 | tf_op jit(solution)/shard_map/all_to_all | solution.py:236
  31.6 0.0 copy-done.1
  31.6 0.0 copy-done.2
  31.6 0.0 copy-done
  31.6 0.5 shard_map.103
  32.1 16.5 %all-gather = bf16[4,96,1152]{2,1,0:T(8,128)(2,1)S(1)} all-gather(bf16[2,96,1152]{2,1,0:T(8,128)(2,1)S(1)} %get-tuple-element.16), channel_id=2, replica_groups={{0,64},{128,192},{256,320},{384,448},{512,576},{640,704},{768,832},{896..., dimensions={0}, use_global_device_ids=true | all-gather | bytes 1327104 | tf_op jit(solution)/shard_map/all_gather | solution.py:250
  48.7 0.1 shard_map.104
  48.7 8.2 %all-gather.1 = bf16[8,24,1152]{2,1,0:T(8,128)(2,1)S(1)} all-gather(bf16[4,24,1152]{2,1,0:T(8,128)(2,1)S(1)} %get-tuple-element.18), channel_id=3, replica_groups={{0,128},{64,192},{256,384},{320,448},{512,640},{576,704},{768,896},{832..., dimensions={0}, use_global_device_ids=true | all-gather | bytes 663552 | tf_op jit(solution)/shard_map/all_gather | solution.py:259
  56.9 25.6 %all_to_all.16.parts_ref = f32[4,24,1152]{2,1,0:T(8,128)S(1)} all-to-all(f32[4,24,1152]{2,1,0:T(8,128)S(1)} %shard_map.105), channel_id=1, replica_groups={{0,256,512,768},{64,320,576,832},{128,384,640,896},{192,448,704,960},{1..., dimensions={0} | all-to-all | bytes 884736 | tf_op jit(solution)/shard_map/all_to_all | solution.py:261
  82.6 33.8 %all-gather.2 = bf16[384,1152]{1,0:T(8,128)(2,1)S(1)} all-gather(bf16[24,1152]{1,0:T(8,128)(2,1)S(1)} %shard_map.106), channel_id=4, replica_groups=mesh['dp'=16,'expert'=64] {'dp'}, dimensions={0}, use_global_device_ids=true | all-gather | bytes 940032 | tf_op jit(solution)/shard_map/all_gather | solution.py:263
  116.4 0.4 shard_map.107
  116.9 24.8 %all_to_all.17 = bf16[64,8,128]{2,1,0:T(8,128)(2,1)S(1)} all-to-all(bf16[64,8,128]{2,1,0:T(8,128)(2,1)S(1)} %bitcast.28), channel_id=1, replica_groups=mesh['dp'=16,'expert'=64] {'expert'}, dimensions={0} | all-to-all | bytes 262144 | tf_op jit(solution)/shard_map/all_to_all | solution.py:266
  141.7 1.6 %shard_map.108 = (bf16[16,256]{1,0:T(8,128)(2,1)}, bf16[256,768]{1,0:T(8,128)(2,1)}, bf16[256,768]{1,0:T(8,128)(2,1)}, bf16[768,256]{1,0:T(8,128)(2,1)}) custom-call(bf16[2,192,1152]{2,1,0:T(8,128)(2,1)S(1)} %bitcast.17, bf16[512,256]{1,0:T(8,128)(2,1)S(1)} %bitcast.20, bf16[32,512]{1,0:T(8,128)(2,1)S(1)} %get-tuple-element.19.back_ref, ...), custom_call_target="tpu_custom_call" | custom-call | flops 226492416 | bytes 2498560 | tf_op jit(solution)/shard_map/pallas_call | solution.py:205
  (2 shorter events, 0.1 us)
Async XLA Ops:
  0.6 31.0 %copy-start.1 = (bf16[1,256,768]{2,1,0:T(8,128)(2,1)S(1)}, bf16[1,256,768]{2,1,0:T(8,128)(2,1)}, u32[]{:S(2)}) copy-start(bf16[1,256,768]{2,1,0:T(8,128)(2,1)} %param.12) | copy-start | bytes 1179652
  0.6 31.0 %copy-start.2 = (bf16[1,768,256]{2,1,0:T(8,128)(2,1)S(1)}, bf16[1,768,256]{2,1,0:T(8,128)(2,1)}, u32[]{:S(2)}) copy-start(bf16[1,768,256]{2,1,0:T(8,128)(2,1)} %param.13) | copy-start | bytes 1179652
  2.0 29.6 %copy-start = (bf16[1,256,768]{2,1,0:T(8,128)(2,1)S(1)}, bf16[1,256,768]{2,1,0:T(8,128)(2,1)}, u32[]{:S(2)}) copy-start(bf16[1,256,768]{2,1,0:T(8,128)(2,1)} %param.11) | copy-start | bytes 1179652

commit v8 on v7

--- a/solution.py
+++ b/solution.py
@@ -135,16 +135,20 @@
         send_ref[i] = (own_ref[i, 1 - mine] + taken_ref[from_partner, i, 1 - mine].astype(F32)).astype(BF16)
 
 
-def second_kernel(own_ref, taken_ref, out_ref):
-    from_partner = 1 - jnp.bitwise_and(lax.shift_right_logical(lax.axis_index("dp"), 1), 1)
-    out_ref[...] = own_ref[...] + taken_ref[from_partner].astype(F32)
-
-
-def activate_body(parts):
-    total = [parts[i] for i in range(QUARTER)]
+def second_kernel(own_ref, taken_ref, out_ref, left_ref):
+    dp = lax.axis_index("dp")
+    from_partner = 1 - jnp.bitwise_and(lax.shift_right_logical(dp, 1), 1)
+    out_ref[...] = (own_ref[...] + taken_ref[from_partner].astype(F32)).astype(BF16)
+    mine = lax.shift_right_logical(dp, 2)
+    kept = own_ref[mine] + taken_ref[from_partner, mine].astype(F32)
+    left_ref[...] = kept - kept.astype(BF16).astype(F32)
+
+
+def activate_body(parts, left):
+    total = [parts[i].astype(F32) for i in range(QUARTER)]
     while len(total) > 1:
         total = [total[i] + total[i + 1] for i in range(0, len(total), 2)]
-    total = total[0]
+    total = total[0] + left
     pre_gate, pre_up, hidden_grad = total[:, :HALF], total[:, HALF : 2 * HALF], total[:, 2 * HALF :]
     sigmoid_gate = jax.nn.sigmoid(pre_gate)
     silu_gate = pre_gate * sigmoid_gate
@@ -154,8 +158,8 @@
     return jnp.concatenate([gate_grad, up_grad, hidden], axis=1).astype(BF16)
 
 
-def activate_kernel(parts_ref, out_ref):
-    out_ref[...] = activate_body(parts_ref[...])
+def activate_kernel(parts_ref, left_ref, out_ref):
+    out_ref[...] = activate_body(parts_ref[...], left_ref[...])
 
 
 def row_grad_body(packed, w_gate, w_up):
@@ -257,9 +261,11 @@
         taken.reshape((2, *eighths)),
     )
     taken = lax.all_gather(send, mesh_axes, axis=0, axis_index_groups=pairs(2))
-    parts = call(second_kernel, [(quarters, F32)], ROWS * PACK // 2, keep, taken)
+    parts, left = call(
+        second_kernel, [(quarters, BF16), ((CHUNK, PACK), F32)], ROWS * PACK // 2, keep, taken
+    )
     parts = lax.all_to_all(parts, "dp", 0, 0, tiled=True, axis_index_groups=FAR)
-    block = call(activate_kernel, [((CHUNK, PACK), BF16)], 20 * CHUNK * PACK, parts)
+    block = call(activate_kernel, [((CHUNK, PACK), BF16)], 20 * CHUNK * PACK, parts, left)
     packed = lax.all_gather(block, "dp", axis=0).reshape(2, ROWS, PACK)
 
     row_grads = call(row_grad_kernel, [((SLOTS, 128), BF16)], 2 * matmul, packed, gate_w, up_w, scratch_shapes=[pltpu.VMEM((SLOTS, 128), F32)])

time: 144 us -> 134 us (0.931)
  blocking collectives: 138 us -> 128 us
    all_gather x1, blocking collectives: 33.8 us -> 26.4 us  [on_device(): packed = lax.all_gather(block, 'dp', axis=0).reshape(2, ROWS, PACK)]
    all_to_all x1, blocking collectives: 25.6 us -> 23.3 us  [on_device(): parts = lax.all_to_all(parts, 'dp', 0, 0, tiled=True, axis_index_groups=FAR)]
where the time goes in v8:
time: 134 us; the launch traced here: 133 us
  blocking collectives  128 us (96%)
  Pallas kernels  4.09 us (3%)
    all_to_all x1, blocking collectives, on_device(): lax.all_to_all(sent.reshape(EXPERTS, 8, WIDTH), 'expert', 0, 0, tiled=True)  29.6 us
    all_gather x1, blocking collectives, on_device(): packed = lax.all_gather(block, 'dp', axis=0).reshape(2, ROWS, PACK)  26.4 us
    all_to_all x1, blocking collectives, on_device(): lax.all_to_all(row_grads.reshape(EXPERTS, 8, 128), 'expert', 0, 0, tiled=...  24.5 us
    all_to_all x1, blocking collectives, on_device(): parts = lax.all_to_all(parts, 'dp', 0, 0, tiled=True, axis_index_groups=FAR)  23.3 us
    all_gather x1, blocking collectives, on_device(): taken = lax.all_gather(send, mesh_axes, axis=0, axis_index_groups=pairs(1))  16.5 us
    all_gather x1, blocking collectives, on_device(): taken = lax.all_gather(send, mesh_axes, axis=0, axis_index_groups=pairs(2))  8.16 us
    pallas_call x7, Pallas kernels, call(): pl.pallas_call(kernel, out_shape=shapes if len(shapes) > 1 else shapes[0]...  4.09 us

profile of v8, /device:TPU:1, one launch (start us, length us, event | category | flops | bytes accessed | tf_op | source)
XLA Modules:
  0.0 133.2 jit_solution(5826010606769370577)
XLA Ops:
  0.6 0.0 copy-start.1
  0.6 0.0 copy-start.2
  0.7 1.4 %shard_map.102 = (bf16[512,256]{1,0:T(8,128)(2,1)S(1)}, bf16[32,512]{1,0:T(8,128)(2,1)S(1)}) custom-call(s32[8,16]{1,0:T(8,128)} %bitcast.34, f32[8,16]{1,0:T(8,128)} %bitcast.35, bf16[16,256]{1,0:T(8,128)(2,1)} %acts.1, bf16[16,256]{1,0:T(8,128)(2,1)} %grad_out.1), custom_call_target="tpu_custom_call" | custom-call | flops 301989888 | bytes 312320 | tf_op jit(solution)/shard_map/pallas_call | solution.py:209
  2.0 0.0 copy-start
  2.1 29.6 %all_to_all.15 = bf16[64,8,256]{2,1,0:T(8,128)(2,1)S(1)} all-to-all(bf16[64,8,256]{2,1,0:T(8,128)(2,1)S(1)} %bitcast.30), channel_id=1, replica_groups=mesh['dp'=16,'expert'=64] {'expert'}, dimensions={0} | all-to-all | bytes 524288 | tf_op jit(solution)/shard_map/all_to_all | solution.py:240
  31.6 0.0 copy-done.1
  31.6 0.0 copy-done.2
  31.6 0.0 copy-done
  31.6 0.5 shard_map.103
  32.1 16.5 %all-gather = bf16[4,96,1152]{2,1,0:T(8,128)(2,1)S(1)} all-gather(bf16[2,96,1152]{2,1,0:T(8,128)(2,1)S(1)} %get-tuple-element.18), channel_id=2, replica_groups={{0,64},{128,192},{256,320},{384,448},{512,576},{640,704},{768,832},{896..., dimensions={0}, use_global_device_ids=true | all-gather | bytes 1327104 | tf_op jit(solution)/shard_map/all_gather | solution.py:254
  48.7 0.1 shard_map.104
  48.7 8.2 %all-gather.1 = bf16[8,24,1152]{2,1,0:T(8,128)(2,1)S(1)} all-gather(bf16[4,24,1152]{2,1,0:T(8,128)(2,1)S(1)} %get-tuple-element.20), channel_id=3, replica_groups={{0,128},{64,192},{256,384},{320,448},{512,640},{576,704},{768,896},{832..., dimensions={0}, use_global_device_ids=true | all-gather | bytes 663552 | tf_op jit(solution)/shard_map/all_gather | solution.py:263
  56.9 0.1 shard_map.105
  57.0 23.3 %all_to_all.16.parts_ref = bf16[4,24,1152]{2,1,0:T(8,128)(2,1)S(1)} all-to-all(bf16[4,24,1152]{2,1,0:T(8,128)(2,1)S(1)} %get-tuple-element.21), channel_id=1, replica_groups={{0,256,512,768},{64,320,576,832},{128,384,640,896},{192,448,704,960},{1..., dimensions={0} | all-to-all | bytes 442368 | tf_op jit(solution)/shard_map/all_to_all | solution.py:267
  80.3 0.1 shard_map.106
  80.3 26.4 %all-gather.2 = bf16[384,1152]{1,0:T(8,128)(2,1)S(1)} all-gather(bf16[24,1152]{1,0:T(8,128)(2,1)S(1)} %shard_map.106), channel_id=4, replica_groups=mesh['dp'=16,'expert'=64] {'dp'}, dimensions={0}, use_global_device_ids=true | all-gather | bytes 940032 | tf_op jit(solution)/shard_map/all_gather | solution.py:269
  106.7 0.4 shard_map.107
  107.2 24.5 %all_to_all.17 = bf16[64,8,128]{2,1,0:T(8,128)(2,1)S(1)} all-to-all(bf16[64,8,128]{2,1,0:T(8,128)(2,1)S(1)} %bitcast.28), channel_id=1, replica_groups=mesh['dp'=16,'expert'=64] {'expert'}, dimensions={0} | all-to-all | bytes 262144 | tf_op jit(solution)/shard_map/all_to_all | solution.py:272
  131.7 1.6 %shard_map.108 = (bf16[16,256]{1,0:T(8,128)(2,1)}, bf16[256,768]{1,0:T(8,128)(2,1)}, bf16[256,768]{1,0:T(8,128)(2,1)}, bf16[768,256]{1,0:T(8,128)(2,1)}) custom-call(bf16[2,192,1152]{2,1,0:T(8,128)(2,1)S(1)} %bitcast.17, bf16[512,256]{1,0:T(8,128)(2,1)S(1)} %bitcast.20, bf16[32,512]{1,0:T(8,128)(2,1)S(1)} %get-tuple-element.23.back_ref, ...), custom_call_target="tpu_custom_call" | custom-call | flops 226492416 | bytes 2498560 | tf_op jit(solution)/shard_map/pallas_call | solution.py:209
Async XLA Ops:
  0.6 31.0 %copy-start.1 = (bf16[1,256,768]{2,1,0:T(8,128)(2,1)S(1)}, bf16[1,256,768]{2,1,0:T(8,128)(2,1)}, u32[]{:S(2)}) copy-start(bf16[1,256,768]{2,1,0:T(8,128)(2,1)} %param.12) | copy-start | bytes 1179652
  0.6 31.0 %copy-start.2 = (bf16[1,768,256]{2,1,0:T(8,128)(2,1)S(1)}, bf16[1,768,256]{2,1,0:T(8,128)(2,1)}, u32[]{:S(2)}) copy-start(bf16[1,768,256]{2,1,0:T(8,128)(2,1)} %param.13) | copy-start | bytes 1179652
  2.0 29.6 %copy-start = (bf16[1,256,768]{2,1,0:T(8,128)(2,1)S(1)}, bf16[1,256,768]{2,1,0:T(8,128)(2,1)}, u32[]{:S(2)}) copy-start(bf16[1,256,768]{2,1,0:T(8,128)(2,1)} %param.11) | copy-start | bytes 1179652

commit v9 on v8

--- a/solution.py
+++ b/solution.py
@@ -56,8 +56,12 @@
     expert = lax.shift_right_logical(iota((TOK, SLOTS), 1), 3)
     hits = [column(routes_t[k : k + 1, :]) == expert for k in range(PICKS)]
     named = functools.reduce(jnp.logical_or, hits)
-    earlier = (iota((TOK, TOK), 0) > iota((TOK, TOK), 1)).astype(F32).astype(BF16)
-    rank = dot(earlier, named.astype(F32).astype(BF16), ((1,), (0,))).astype(jnp.int32)
+    counts = named.astype(F32)
+    row = iota((TOK, SLOTS), 0)
+    running = counts
+    for step in (1, 2, 4, 8):
+        running += jnp.where(row >= step, jnp.roll(running, step, axis=0), 0.0)
+    rank = (running - counts).astype(jnp.int32)
     return hits, named, rank
 
 
@@ -117,8 +121,10 @@
     return jnp.where(is_odd, odd, even), jnp.where(is_odd, even, odd)
 
 
-def product_kernel(received_ref, w_gate_ref, w_up_ref, w_down_ref, own_ref, send_ref, held):
+def product_kernel(received_ref, w_gate_ref, w_up_ref, w_down_ref, own_ref, send_ref, x_ref, dy_ref, held):
     rows_x, rows_dy = take_rows(received_ref, held)
+    x_ref[...] = rows_x
+    dy_ref[...] = rows_dy
     parity = jnp.bitwise_and(lax.axis_index("dp"), 1)
     for half, both in enumerate(products(rows_x, rows_dy, w_gate_ref[...], w_up_ref[...], w_down_ref[...])):
         own, other = split_rows(both, parity)
@@ -183,8 +189,7 @@
     out_ref[...] = held[...].astype(BF16)
 
 
-def weight_kernel(packed_ref, received_ref, gate_ref, up_ref, down_ref, held):
-    rows_x, rows_dy = take_rows(received_ref, held)
+def weight_products(packed_ref, rows_x, rows_dy, gate_ref, up_ref, down_ref):
     for half in range(2):
         cut = slice(half * HALF, (half + 1) * HALF)
         gate_ref[:, cut] = dot(rows_x, packed_ref[half, :, :HALF], ((0,), (0,))).astype(BF16)
@@ -198,9 +203,9 @@
     return jnp.concatenate([left, right], axis=1).astype(BF16)
 
 
-def final_kernel(packed_ref, received_ref, back_ref, returned_ref, acts_ref, gate_ref, up_ref, down_ref, held):
+def final_kernel(packed_ref, x_ref, dy_ref, back_ref, returned_ref, acts_ref, gate_ref, up_ref, down_ref):
     acts_ref[...] = combine_body(back_ref[...], returned_ref[...])
-    weight_kernel(packed_ref, received_ref, gate_ref, up_ref, down_ref, held)
+    weight_products(packed_ref, x_ref[...], dy_ref[...], gate_ref, up_ref, down_ref)
 
 
 def call(kernel, outs, flops, *operands, **options):
@@ -240,9 +245,9 @@
     received = lax.all_to_all(sent.reshape(EXPERTS, 8, WIDTH), "expert", 0, 0, tiled=True)
     received = received.reshape(SLOTS, WIDTH)
 
-    own, send = call(
+    own, send, rows_x, rows_dy = call(
         product_kernel,
-        [((2, ROWS // 2, PACK), F32), ((2, ROWS // 2, PACK), BF16)],
+        [((2, ROWS // 2, PACK), F32), ((2, ROWS // 2, PACK), BF16), ((ROWS, WIDTH), BF16), ((ROWS, WIDTH), BF16)],
         3 * matmul,
         received,
         gate_w,
@@ -275,10 +280,10 @@
         [((TOK, WIDTH), BF16), ((WIDTH, HIDDEN), BF16), ((WIDTH, HIDDEN), BF16), ((HIDDEN, WIDTH), BF16)],
         3 * matmul,
         packed,
-        received,
+        rows_x,
+        rows_dy,
         back,
         returned.reshape(SLOTS, 128),
-        scratch_shapes=[TAKEN],
     )
     return grad_acts, new_gate[None], new_up[None], new_down[None]
 

time: 134 us -> 133 us (level)
  no operation moved by 1% of the time
where the time goes in v9:
time: 133 us
  blocking collectives  129 us (97%)
  Pallas kernels  3.97 us (3%)
    all_to_all x1, blocking collectives, on_device(): lax.all_to_all(sent.reshape(EXPERTS, 8, WIDTH), 'expert', 0, 0, tiled=True)  29.6 us
    all_gather x1, blocking collectives, on_device(): packed = lax.all_gather(block, 'dp', axis=0).reshape(2, ROWS, PACK)  26.4 us
    all_to_all x1, blocking collectives, on_device(): lax.all_to_all(row_grads.reshape(EXPERTS, 8, 128), 'expert', 0, 0, tiled=...  24.6 us
    all_to_all x1, blocking collectives, on_device(): parts = lax.all_to_all(parts, 'dp', 0, 0, tiled=True, axis_index_groups=FAR)  23.3 us
    all_gather x1, blocking collectives, on_device(): taken = lax.all_gather(send, mesh_axes, axis=0, axis_index_groups=pairs(1))  16.5 us
    all_gather x1, blocking collectives, on_device(): taken = lax.all_gather(send, mesh_axes, axis=0, axis_index_groups=pairs(2))  8.16 us
    pallas_call x7, Pallas kernels, call(): pl.pallas_call(kernel, out_shape=shapes if len(shapes) > 1 else shapes[0]...  3.97 us

profile of v9, /device:TPU:1, one launch (start us, length us, event | category | flops | bytes accessed | tf_op | source)
XLA Modules:
  0.0 133.2 jit_solution(3760973753552098893)
XLA Ops:
  0.6 0.0 copy-start.1
  0.6 0.0 copy-start.2
  0.7 1.3 shard_map.102
  1.9 0.0 copy-start
  1.9 29.6 %all_to_all.15 = bf16[64,8,256]{2,1,0:T(8,128)(2,1)S(1)} all-to-all(bf16[64,8,256]{2,1,0:T(8,128)(2,1)S(1)} %bitcast.29), channel_id=1, replica_groups=mesh['dp'=16,'expert'=64] {'expert'}, dimensions={0} | all-to-all | bytes 524288 | tf_op jit(solution)/shard_map/all_to_all | solution.py:245
  31.5 0.0 copy-done.1
  31.5 0.0 copy-done.2
  31.5 0.0 copy-done
  31.5 0.5 shard_map.103
  32.0 16.5 %all-gather = bf16[4,96,1152]{2,1,0:T(8,128)(2,1)S(1)} all-gather(bf16[2,96,1152]{2,1,0:T(8,128)(2,1)S(1)} %get-tuple-element.20), channel_id=2, replica_groups={{0,64},{128,192},{256,320},{384,448},{512,576},{640,704},{768,832},{896..., dimensions={0}, use_global_device_ids=true | all-gather | bytes 1327104 | tf_op jit(solution)/shard_map/all_gather | solution.py:259
  48.5 0.1 shard_map.104
  48.6 8.2 %all-gather.1 = bf16[8,24,1152]{2,1,0:T(8,128)(2,1)S(1)} all-gather(bf16[4,24,1152]{2,1,0:T(8,128)(2,1)S(1)} %get-tuple-element.22), channel_id=3, replica_groups={{0,128},{64,192},{256,384},{320,448},{512,640},{576,704},{768,896},{832..., dimensions={0}, use_global_device_ids=true | all-gather | bytes 663552 | tf_op jit(solution)/shard_map/all_gather | solution.py:268
  56.8 0.1 shard_map.105
  56.9 23.3 %all_to_all.16.parts_ref = bf16[4,24,1152]{2,1,0:T(8,128)(2,1)S(1)} all-to-all(bf16[4,24,1152]{2,1,0:T(8,128)(2,1)S(1)} %get-tuple-element.23), channel_id=1, replica_groups={{0,256,512,768},{64,320,576,832},{128,384,640,896},{192,448,704,960},{1..., dimensions={0} | all-to-all | bytes 442368 | tf_op jit(solution)/shard_map/all_to_all | solution.py:272
  80.2 0.1 shard_map.106
  80.2 26.4 %all-gather.2 = bf16[384,1152]{1,0:T(8,128)(2,1)S(1)} all-gather(bf16[24,1152]{1,0:T(8,128)(2,1)S(1)} %shard_map.106), channel_id=4, replica_groups=mesh['dp'=16,'expert'=64] {'dp'}, dimensions={0}, use_global_device_ids=true | all-gather | bytes 940032 | tf_op jit(solution)/shard_map/all_gather | solution.py:274
  106.6 0.4 shard_map.107
  107.1 24.6 %all_to_all.17 = bf16[64,8,128]{2,1,0:T(8,128)(2,1)S(1)} all-to-all(bf16[64,8,128]{2,1,0:T(8,128)(2,1)S(1)} %bitcast.27), channel_id=1, replica_groups=mesh['dp'=16,'expert'=64] {'expert'}, dimensions={0} | all-to-all | bytes 262144 | tf_op jit(solution)/shard_map/all_to_all | solution.py:277
  131.7 1.5 %shard_map.108 = (bf16[16,256]{1,0:T(8,128)(2,1)}, bf16[256,768]{1,0:T(8,128)(2,1)}, bf16[256,768]{1,0:T(8,128)(2,1)}, bf16[768,256]{1,0:T(8,128)(2,1)}) custom-call(bf16[2,192,1152]{2,1,0:T(8,128)(2,1)S(1)} %bitcast.17, bf16[192,256]{1,0:T(8,128)(2,1)S(1)} %get-tuple-element.25.x_ref, bf16[192,256]{1,0:T(8,128)(2,1)S(1)} %get-tuple-element.26.dy_ref, ...), custom_call_target="tpu_custom_call" | custom-call | flops 226492416 | bytes 2433024 | tf_op jit(solution)/shard_map/pallas_call | solution.py:214
Async XLA Ops:
  0.6 30.9 %copy-start.1 = (bf16[1,256,768]{2,1,0:T(8,128)(2,1)S(1)}, bf16[1,256,768]{2,1,0:T(8,128)(2,1)}, u32[]{:S(2)}) copy-start(bf16[1,256,768]{2,1,0:T(8,128)(2,1)} %param.12) | copy-start | bytes 1179652
  0.6 30.9 %copy-start.2 = (bf16[1,768,256]{2,1,0:T(8,128)(2,1)S(1)}, bf16[1,768,256]{2,1,0:T(8,128)(2,1)}, u32[]{:S(2)}) copy-start(bf16[1,768,256]{2,1,0:T(8,128)(2,1)} %param.13) | copy-start | bytes 1179652
  1.9 29.6 %copy-start = (bf16[1,256,768]{2,1,0:T(8,128)(2,1)S(1)}, bf16[1,256,768]{2,1,0:T(8,128)(2,1)}, u32[]{:S(2)}) copy-start(bf16[1,256,768]{2,1,0:T(8,128)(2,1)} %param.11) | copy-start | bytes 1179652

commit v10 on v9

--- a/solution.py
+++ b/solution.py
@@ -123,8 +123,8 @@
 
 def product_kernel(received_ref, w_gate_ref, w_up_ref, w_down_ref, own_ref, send_ref, x_ref, dy_ref, held):
     rows_x, rows_dy = take_rows(received_ref, held)
-    x_ref[...] = rows_x
-    dy_ref[...] = rows_dy
+    x_ref[...] = reorder(rows_x.astype(F32)).astype(BF16)
+    dy_ref[...] = reorder(rows_dy.astype(F32)).astype(BF16)
     parity = jnp.bitwise_and(lax.axis_index("dp"), 1)
     for half, both in enumerate(products(rows_x, rows_dy, w_gate_ref[...], w_up_ref[...], w_down_ref[...])):
         own, other = split_rows(both, parity)
@@ -141,20 +141,16 @@
         send_ref[i] = (own_ref[i, 1 - mine] + taken_ref[from_partner, i, 1 - mine].astype(F32)).astype(BF16)
 
 
-def second_kernel(own_ref, taken_ref, out_ref, left_ref):
-    dp = lax.axis_index("dp")
-    from_partner = 1 - jnp.bitwise_and(lax.shift_right_logical(dp, 1), 1)
-    out_ref[...] = (own_ref[...] + taken_ref[from_partner].astype(F32)).astype(BF16)
-    mine = lax.shift_right_logical(dp, 2)
-    kept = own_ref[mine] + taken_ref[from_partner, mine].astype(F32)
-    left_ref[...] = kept - kept.astype(BF16).astype(F32)
-
-
-def activate_body(parts, left):
-    total = [parts[i].astype(F32) for i in range(QUARTER)]
-    while len(total) > 1:
-        total = [total[i] + total[i + 1] for i in range(0, len(total), 2)]
-    total = total[0] + left
+def second_kernel(own_ref, taken_ref, out_ref, sum_ref):
+    from_partner = 1 - jnp.bitwise_and(lax.shift_right_logical(lax.axis_index("dp"), 1), 1)
+    total = own_ref[...] + taken_ref[from_partner].astype(F32)
+    sum_ref[...] = total
+    out_ref[...] = total.astype(BF16)
+
+
+def activate_body(parts, own):
+    wide = [part.astype(F32) for part in parts]
+    total = (wide[0] + wide[1]) + (wide[2] + wide[3]) + (own - own.astype(BF16).astype(F32))
     pre_gate, pre_up, hidden_grad = total[:, :HALF], total[:, HALF : 2 * HALF], total[:, 2 * HALF :]
     sigmoid_gate = jax.nn.sigmoid(pre_gate)
     silu_gate = pre_gate * sigmoid_gate
@@ -164,21 +160,30 @@
     return jnp.concatenate([gate_grad, up_grad, hidden], axis=1).astype(BF16)
 
 
-def activate_kernel(parts_ref, left_ref, out_ref):
-    out_ref[...] = activate_body(parts_ref[...], left_ref[...])
-
-
-def row_grad_body(packed, w_gate, w_up):
+def activate_kernel(parts_ref, sum_ref, out_ref):
+    for i in range(QUARTER):
+        out_ref[i] = activate_body([parts_ref[k, i] for k in range(QUARTER)], sum_ref[i])
+
+
+def reorder(rows):
+    return jnp.concatenate([rows[CHUNK * i : CHUNK * (i + 1)] for i in (0, 4, 2, 6, 1, 5, 3, 7)], axis=0)
+
+
+def half_of(packed_ref, half, first, last):
+    return jnp.concatenate([packed_ref[i, half, :, first:last] for i in range(4)], axis=0)
+
+
+def row_grad_body(packed_ref, w_gate, w_up):
     total = jnp.zeros((ROWS, WIDTH), F32)
     for half in range(2):
         cut = slice(half * HALF, (half + 1) * HALF)
-        total += dot(packed[half][:, :HALF], w_gate[:, cut], ((1,), (1,)))
-        total += dot(packed[half][:, HALF : 2 * HALF], w_up[:, cut], ((1,), (1,)))
-    return total
+        total += dot(half_of(packed_ref, half, 0, HALF), w_gate[:, cut], ((1,), (1,)))
+        total += dot(half_of(packed_ref, half, HALF, 2 * HALF), w_up[:, cut], ((1,), (1,)))
+    return reorder(total)
 
 
 def row_grad_kernel(packed_ref, w_gate_ref, w_up_ref, out_ref, held):
-    total = row_grad_body(packed_ref[...], w_gate_ref[...], w_up_ref[...])
+    total = row_grad_body(packed_ref, w_gate_ref[...], w_up_ref[...])
     for place in range(8):
         slot, half = divmod(place, 2)
         if slot < CAP:
@@ -192,9 +197,9 @@
 def weight_products(packed_ref, rows_x, rows_dy, gate_ref, up_ref, down_ref):
     for half in range(2):
         cut = slice(half * HALF, (half + 1) * HALF)
-        gate_ref[:, cut] = dot(rows_x, packed_ref[half, :, :HALF], ((0,), (0,))).astype(BF16)
-        up_ref[:, cut] = dot(rows_x, packed_ref[half, :, HALF : 2 * HALF], ((0,), (0,))).astype(BF16)
-        down_ref[cut, :] = dot(packed_ref[half, :, 2 * HALF :], rows_dy, ((0,), (0,))).astype(BF16)
+        gate_ref[:, cut] = dot(rows_x, half_of(packed_ref, half, 0, HALF), ((0,), (0,))).astype(BF16)
+        up_ref[:, cut] = dot(rows_x, half_of(packed_ref, half, HALF, 2 * HALF), ((0,), (0,))).astype(BF16)
+        down_ref[cut, :] = dot(half_of(packed_ref, half, 2 * HALF, PACK), rows_dy, ((0,), (0,))).astype(BF16)
 
 
 def combine_body(back, returned):
@@ -266,12 +271,11 @@
         taken.reshape((2, *eighths)),
     )
     taken = lax.all_gather(send, mesh_axes, axis=0, axis_index_groups=pairs(2))
-    parts, left = call(
-        second_kernel, [(quarters, BF16), ((CHUNK, PACK), F32)], ROWS * PACK // 2, keep, taken
-    )
-    parts = lax.all_to_all(parts, "dp", 0, 0, tiled=True, axis_index_groups=FAR)
-    block = call(activate_kernel, [((CHUNK, PACK), BF16)], 20 * CHUNK * PACK, parts, left)
-    packed = lax.all_gather(block, "dp", axis=0).reshape(2, ROWS, PACK)
+    parts, total = call(second_kernel, [(quarters, BF16), (quarters, F32)], ROWS * PACK // 2, keep, taken)
+    parts = lax.all_gather(parts, "dp", axis=0, axis_index_groups=FAR)
+    block = call(activate_kernel, [(quarters, BF16)], 80 * CHUNK * PACK, parts, total)
+    block = lax.all_gather(block, mesh_axes, axis=0, axis_index_groups=pairs(2))
+    packed = lax.all_gather(block, mesh_axes, axis=0, axis_index_groups=pairs(1)).reshape(4, 2, 2 * CHUNK, PACK)
 
     row_grads = call(row_grad_kernel, [((SLOTS, 128), BF16)], 2 * matmul, packed, gate_w, up_w, scratch_shapes=[pltpu.VMEM((SLOTS, 128), F32)])
     returned = lax.all_to_all(row_grads.reshape(EXPERTS, 8, 128), "expert", 0, 0, tiled=True)

time: 133 us -> 132 us (level)
  blocking collectives: 129 us -> 127 us
    all_gather x1 -> x3, blocking collectives: 26.4 us -> 53.8 us  [the longest x1 33.8 us: on_device(): parts = lax.all_gather(parts, 'dp', axis=0, axis_index_groups=FAR)]
    all_to_all x1 -> x0, blocking collectives: 23.3 us -> none  [on_device(): parts = lax.all_to_all(parts, 'dp', 0, 0, tiled=True, axis_index_groups=FAR)]
    all_to_all x1, blocking collectives: 24.6 us -> 18.8 us  [on_device(): lax.all_to_all(row_grads.reshape(EXPERTS, 8, 128), 'expert', 0, 0, tiled=...]
where the time goes in v10:
time: 132 us
  blocking collectives  127 us (96%)
  Pallas kernels  4.12 us (3%)
    all_gather x1, blocking collectives, on_device(): parts = lax.all_gather(parts, 'dp', axis=0, axis_index_groups=FAR)  33.8 us
    all_to_all x1, blocking collectives, on_device(): lax.all_to_all(sent.reshape(EXPERTS, 8, WIDTH), 'expert', 0, 0, tiled=True)  29.6 us
    all_to_all x1, blocking collectives, on_device(): lax.all_to_all(row_grads.reshape(EXPERTS, 8, 128), 'expert', 0, 0, tiled=...  18.8 us
    all_gather x1, blocking collectives, on_device(): taken = lax.all_gather(send, mesh_axes, axis=0, axis_index_groups=pairs(1))  16.5 us
    all_gather x1, blocking collectives, on_device(): lax.all_gather(block, mesh_axes, axis=0, axis_index_groups=pairs(1))  12 us
    all_gather x1, blocking collectives, on_device(): taken = lax.all_gather(send, mesh_axes, axis=0, axis_index_groups=pairs(2))  8.16 us
    all_gather x1, blocking collectives, on_device(): block = lax.all_gather(block, mesh_axes, axis=0, axis_index_groups=pairs(2))  7.97 us
    pallas_call x7, Pallas kernels, call(): pl.pallas_call(kernel, out_shape=shapes if len(shapes) > 1 else shapes[0]...  4.12 us

profile of v10, /device:TPU:1, one launch (start us, length us, event | category | flops | bytes accessed | tf_op | source)
XLA Modules:
  0.0 131.7 jit_solution(12007128171082312028)
XLA Ops:
  0.6 0.0 copy-start.1
  0.6 0.0 copy-start.2
  0.7 1.3 shard_map.102
  1.9 0.0 copy-start
  1.9 29.6 %all_to_all.10 = bf16[64,8,256]{2,1,0:T(8,128)(2,1)S(1)} all-to-all(bf16[64,8,256]{2,1,0:T(8,128)(2,1)S(1)} %bitcast.32), channel_id=1, replica_groups=mesh['dp'=16,'expert'=64] {'expert'}, dimensions={0} | all-to-all | bytes 524288 | tf_op jit(solution)/shard_map/all_to_all | solution.py:250
  31.5 0.0 copy-done.1
  31.5 0.0 copy-done.2
  31.5 0.0 copy-done
  31.5 0.5 shard_map.103
  32.0 16.5 %all-gather = bf16[4,96,1152]{2,1,0:T(8,128)(2,1)S(1)} all-gather(bf16[2,96,1152]{2,1,0:T(8,128)(2,1)S(1)} %get-tuple-element.20), channel_id=2, replica_groups={{0,64},{128,192},{256,320},{384,448},{512,576},{640,704},{768,832},{896..., dimensions={0}, use_global_device_ids=true | all-gather | bytes 1327104 | tf_op jit(solution)/shard_map/all_gather | solution.py:264
  48.5 0.1 shard_map.104
  48.6 8.2 %all-gather.1 = bf16[8,24,1152]{2,1,0:T(8,128)(2,1)S(1)} all-gather(bf16[4,24,1152]{2,1,0:T(8,128)(2,1)S(1)} %get-tuple-element.22), channel_id=3, replica_groups={{0,128},{64,192},{256,384},{320,448},{512,640},{576,704},{768,896},{832..., dimensions={0}, use_global_device_ids=true | all-gather | bytes 663552 | tf_op jit(solution)/shard_map/all_gather | solution.py:273
  56.8 0.1 shard_map.105
  56.9 33.8 %all-gather.2 = bf16[16,24,1152]{2,1,0:T(8,128)(2,1)S(1)} all-gather(bf16[4,24,1152]{2,1,0:T(8,128)(2,1)S(1)} %get-tuple-element.23), channel_id=4, replica_groups={{0,256,512,768},{64,320,576,832},{128,384,640,896},{192,448,704,960},{1..., dimensions={0}, use_global_device_ids=true | all-gather | bytes 1105920 | tf_op jit(solution)/shard_map/all_gather | solution.py:275
  90.7 0.2 shard_map.106
  90.9 8.0 %all-gather.3 = bf16[8,24,1152]{2,1,0:T(8,128)(2,1)S(1)} all-gather(bf16[4,24,1152]{2,1,0:T(8,128)(2,1)S(1)} %shard_map.106), channel_id=5, replica_groups={{0,128},{64,192},{256,384},{320,448},{512,640},{576,704},{768,896},{832..., dimensions={0}, use_global_device_ids=true | all-gather | bytes 663552 | tf_op jit(solution)/shard_map/all_gather | solution.py:277
  98.9 12.0 %all-gather.4 = bf16[4,4,24,1152]{3,2,1,0:T(8,128)(2,1)S(1)} all-gather(bf16[2,4,24,1152]{3,2,1,0:T(8,128)(2,1)S(1)} %bitcast.33), channel_id=6, replica_groups={{0,64},{128,192},{256,320},{384,448},{512,576},{640,704},{768,832},{896..., dimensions={0}, use_global_device_ids=true | all-gather | bytes 1327104 | tf_op jit(solution)/shard_map/all_gather | solution.py:278
  110.9 0.4 shard_map.107
  111.3 18.8 %all_to_all.11 = bf16[64,8,128]{2,1,0:T(8,128)(2,1)S(1)} all-to-all(bf16[64,8,128]{2,1,0:T(8,128)(2,1)S(1)} %bitcast.30), channel_id=1, replica_groups=mesh['dp'=16,'expert'=64] {'expert'}, dimensions={0} | all-to-all | bytes 262144 | tf_op jit(solution)/shard_map/all_to_all | solution.py:281
  130.2 1.5 %shard_map.108 = (bf16[16,256]{1,0:T(8,128)(2,1)}, bf16[256,768]{1,0:T(8,128)(2,1)}, bf16[256,768]{1,0:T(8,128)(2,1)}, bf16[768,256]{1,0:T(8,128)(2,1)}) custom-call(bf16[4,2,48,1152]{3,2,1,0:T(8,128)(2,1)S(1)} %bitcast.19, bf16[192,256]{1,0:T(8,128)(2,1)S(1)} %get-tuple-element.25.x_ref, bf16[192,256]{1,0:T(8,128)(2,1)S(1)} %get-tuple-element.26.dy_ref, ...), custom_call_target="tpu_custom_call" | custom-call | flops 226492416 | bytes 2433024 | tf_op jit(solution)/shard_map/pallas_call | solution.py:219
Async XLA Ops:
  0.6 30.9 %copy-start.1 = (bf16[1,256,768]{2,1,0:T(8,128)(2,1)S(1)}, bf16[1,256,768]{2,1,0:T(8,128)(2,1)}, u32[]{:S(2)}) copy-start(bf16[1,256,768]{2,1,0:T(8,128)(2,1)} %param.12) | copy-start | bytes 1179652
  0.6 30.9 %copy-start.2 = (bf16[1,768,256]{2,1,0:T(8,128)(2,1)S(1)}, bf16[1,768,256]{2,1,0:T(8,128)(2,1)}, u32[]{:S(2)}) copy-start(bf16[1,768,256]{2,1,0:T(8,128)(2,1)} %param.13) | copy-start | bytes 1179652
  1.9 29.6 %copy-start = (bf16[1,256,768]{2,1,0:T(8,128)(2,1)S(1)}, bf16[1,256,768]{2,1,0:T(8,128)(2,1)}, u32[]{:S(2)}) copy-start(bf16[1,256,768]{2,1,0:T(8,128)(2,1)} %param.11) | copy-start | bytes 1179652

commit v11 on v10

--- a/solution.py
+++ b/solution.py
@@ -25,6 +25,13 @@
 FAR = [[4 * a + low for a in range(QUARTER)] for low in range(4)]
 
 
+NEAR = [
+    [(4 * first + 2 * (expert % 2) + i) % DP * EXPERTS + expert for i in range(4)]
+    for expert in range(EXPERTS)
+    for first in range(QUARTER)
+]
+
+
 def pairs(distance):
     firsts = [dp for dp in range(DP) if not dp & distance]
     sign = [distance, -distance]
@@ -170,7 +177,9 @@
 
 
 def half_of(packed_ref, half, first, last):
-    return jnp.concatenate([packed_ref[i, half, :, first:last] for i in range(4)], axis=0)
+    flip = 2 * jnp.bitwise_and(lax.axis_index("expert"), 1)
+    places = [jnp.bitwise_xor(flip, low) for low in (0, 2, 1, 3)]
+    return jnp.concatenate([packed_ref[place, half, :, first:last] for place in places], axis=0)
 
 
 def row_grad_body(packed_ref, w_gate, w_up):
@@ -274,8 +283,7 @@
     parts, total = call(second_kernel, [(quarters, BF16), (quarters, F32)], ROWS * PACK // 2, keep, taken)
     parts = lax.all_gather(parts, "dp", axis=0, axis_index_groups=FAR)
     block = call(activate_kernel, [(quarters, BF16)], 80 * CHUNK * PACK, parts, total)
-    block = lax.all_gather(block, mesh_axes, axis=0, axis_index_groups=pairs(2))
-    packed = lax.all_gather(block, mesh_axes, axis=0, axis_index_groups=pairs(1)).reshape(4, 2, 2 * CHUNK, PACK)
+    packed = lax.all_gather(block, mesh_axes, axis=0, axis_index_groups=NEAR).reshape(4, 2, 2 * CHUNK, PACK)
 
     row_grads = call(row_grad_kernel, [((SLOTS, 128), BF16)], 2 * matmul, packed, gate_w, up_w, scratch_shapes=[pltpu.VMEM((SLOTS, 128), F32)])
     returned = lax.all_to_all(row_grads.reshape(EXPERTS, 8, 128), "expert", 0, 0, tiled=True)

time: 132 us -> 134 us (1.015)
    all_to_all x1, blocking collectives: 18.8 us -> 23.3 us  [on_device(): lax.all_to_all(row_grads.reshape(EXPERTS, 8, 128), 'expert', 0, 0, tiled=...]
    all_gather x2 -> x1, blocking collectives: 19.9 us -> 17 us  [on_device(): lax.all_gather(block, mesh_axes, axis=0, axis_index_groups=NEAR)]
where the time goes in v11:
time: 134 us; the launch traced here: 133 us
  blocking collectives  128 us (96%)
  Pallas kernels  4.12 us (3%)
    all_gather x1, blocking collectives, on_device(): parts = lax.all_gather(parts, 'dp', axis=0, axis_index_groups=FAR)  33.8 us
    all_to_all x1, blocking collectives, on_device(): lax.all_to_all(sent.reshape(EXPERTS, 8, WIDTH), 'expert', 0, 0, tiled=True)  29.6 us
    all_to_all x1, blocking collectives, on_device(): lax.all_to_all(row_grads.reshape(EXPERTS, 8, 128), 'expert', 0, 0, tiled=...  23.3 us
    all_gather x1, blocking collectives, on_device(): lax.all_gather(block, mesh_axes, axis=0, axis_index_groups=NEAR)  17 us
    all_gather x1, blocking collectives, on_device(): taken = lax.all_gather(send, mesh_axes, axis=0, axis_index_groups=pairs(1))  16.5 us
    all_gather x1, blocking collectives, on_device(): taken = lax.all_gather(send, mesh_axes, axis=0, axis_index_groups=pairs(2))  8.16 us
    pallas_call x7, Pallas kernels, call(): pl.pallas_call(kernel, out_shape=shapes if len(shapes) > 1 else shapes[0]...  4.12 us

profile of v11, /device:TPU:1, one launch (start us, length us, event | category | flops | bytes accessed | tf_op | source)
XLA Modules:
  0.0 133.3 jit_solution(1629081012400670814)
XLA Ops:
  0.6 0.0 copy-start.1
  0.6 0.0 copy-start.2
  0.7 1.3 shard_map.102
  1.9 0.0 copy-start
  1.9 29.6 %all_to_all.10 = bf16[64,8,256]{2,1,0:T(8,128)(2,1)S(1)} all-to-all(bf16[64,8,256]{2,1,0:T(8,128)(2,1)S(1)} %bitcast.31), channel_id=1, replica_groups=mesh['dp'=16,'expert'=64] {'expert'}, dimensions={0} | all-to-all | bytes 524288 | tf_op jit(solution)/shard_map/all_to_all | solution.py:259
  31.5 0.0 copy-done.1
  31.5 0.0 copy-done.2
  31.5 0.0 copy-done
  31.5 0.5 shard_map.103
  32.0 16.5 %all-gather = bf16[4,96,1152]{2,1,0:T(8,128)(2,1)S(1)} all-gather(bf16[2,96,1152]{2,1,0:T(8,128)(2,1)S(1)} %get-tuple-element.20), channel_id=2, replica_groups={{0,64},{128,192},{256,320},{384,448},{512,576},{640,704},{768,832},{896..., dimensions={0}, use_global_device_ids=true | all-gather | bytes 1327104 | tf_op jit(solution)/shard_map/all_gather | solution.py:273
  48.5 0.1 shard_map.104
  48.6 8.2 %all-gather.1 = bf16[8,24,1152]{2,1,0:T(8,128)(2,1)S(1)} all-gather(bf16[4,24,1152]{2,1,0:T(8,128)(2,1)S(1)} %get-tuple-element.22), channel_id=3, replica_groups={{0,128},{64,192},{256,384},{320,448},{512,640},{576,704},{768,896},{832..., dimensions={0}, use_global_device_ids=true | all-gather | bytes 663552 | tf_op jit(solution)/shard_map/all_gather | solution.py:282
  56.8 0.1 shard_map.105
  56.9 33.8 %all-gather.2 = bf16[16,24,1152]{2,1,0:T(8,128)(2,1)S(1)} all-gather(bf16[4,24,1152]{2,1,0:T(8,128)(2,1)S(1)} %get-tuple-element.23), channel_id=4, replica_groups={{0,256,512,768},{64,320,576,832},{128,384,640,896},{192,448,704,960},{1..., dimensions={0}, use_global_device_ids=true | all-gather | bytes 1105920 | tf_op jit(solution)/shard_map/all_gather | solution.py:284
  90.7 0.2 shard_map.106
  90.9 17.0 %all-gather.3 = bf16[16,24,1152]{2,1,0:T(8,128)(2,1)S(1)} all-gather(bf16[4,24,1152]{2,1,0:T(8,128)(2,1)S(1)} %shard_map.106), channel_id=5, replica_groups={{0,64,128,192},{256,320,384,448},{512,576,640,704},{768,832,896,960},{1..., dimensions={0}, use_global_device_ids=true | all-gather | bytes 1105920 | tf_op jit(solution)/shard_map/all_gather | solution.py:286
  107.9 0.4 shard_map.107
  108.4 23.3 %all_to_all.11 = bf16[64,8,128]{2,1,0:T(8,128)(2,1)S(1)} all-to-all(bf16[64,8,128]{2,1,0:T(8,128)(2,1)S(1)} %bitcast.29), channel_id=1, replica_groups=mesh['dp'=16,'expert'=64] {'expert'}, dimensions={0} | all-to-all | bytes 262144 | tf_op jit(solution)/shard_map/all_to_all | solution.py:289
  131.7 1.5 %shard_map.108 = (bf16[16,256]{1,0:T(8,128)(2,1)}, bf16[256,768]{1,0:T(8,128)(2,1)}, bf16[256,768]{1,0:T(8,128)(2,1)}, bf16[768,256]{1,0:T(8,128)(2,1)}) custom-call(bf16[4,2,48,1152]{3,2,1,0:T(8,128)(2,1)S(1)} %bitcast.18, bf16[192,256]{1,0:T(8,128)(2,1)S(1)} %get-tuple-element.25.x_ref, bf16[192,256]{1,0:T(8,128)(2,1)S(1)} %get-tuple-element.26.dy_ref, ...), custom_call_target="tpu_custom_call" | custom-call | flops 226492416 | bytes 2433024 | tf_op jit(solution)/shard_map/pallas_call | solution.py:228
Async XLA Ops:
  0.6 30.9 %copy-start.1 = (bf16[1,256,768]{2,1,0:T(8,128)(2,1)S(1)}, bf16[1,256,768]{2,1,0:T(8,128)(2,1)}, u32[]{:S(2)}) copy-start(bf16[1,256,768]{2,1,0:T(8,128)(2,1)} %param.12) | copy-start | bytes 1179652
  0.6 30.9 %copy-start.2 = (bf16[1,768,256]{2,1,0:T(8,128)(2,1)S(1)}, bf16[1,768,256]{2,1,0:T(8,128)(2,1)}, u32[]{:S(2)}) copy-start(bf16[1,768,256]{2,1,0:T(8,128)(2,1)} %param.13) | copy-start | bytes 1179652
  1.9 29.6 %copy-start = (bf16[1,256,768]{2,1,0:T(8,128)(2,1)S(1)}, bf16[1,256,768]{2,1,0:T(8,128)(2,1)}, u32[]{:S(2)}) copy-start(bf16[1,256,768]{2,1,0:T(8,128)(2,1)} %param.11) | copy-start | bytes 1179652
